TPU v7x, 128 devices: a whole 4x4x4 slice. The times are simulated.
128 devices in a mesh: row: 8 (over x_lo, y), col: 16 (over x_hi, z, core).
Axes of the slice: x: 4 (x_hi: 2, x_lo: 2; x = x_hi * 2 + x_lo), y: 4, z: 4, core: 2. Of those that a mesh axis runs over, the one named last changes fastest.
Arguments:
- perturbations: float32 [512, 16384], P('row', 'col'), may hold values from -200 to 200
- probes: float32 [16384, 128], P(('col', 'row')), may hold values from -6 to 6
Outputs:
- localized: float32 [16384, 8192], P('col', 'row')
- sampled: float32 [16384, 128], P(('col', 'row'))
All inputs are finite; a program needn't handle non-finite values.
Results may differ from a plain program's by a relative error of at most 0.00013.
Values sent between devices are 32-bit elements; how exact they have to be, the bound alone decides.
A program may use at most 128 MiB of HBM per device.

v0:
```python
import math

import jax
import jax.numpy as jnp
from jax import lax
from jax.sharding import Mesh
from jax.sharding import PartitionSpec as P

MEMBERS = 512
STEPS = 3
ROW = ("row_0", "row_1")
COL = ("col_0", "col_1", "col_2")
ROW_COL = ("row_0", "row_1", "col_0", "col_1", "col_2")
COL_ROW = ("col_0", "col_1", "col_2", "row_0", "row_1")


epsilon = 1e-06
power_terms = (
    2.0 / math.pi - 4.0 / (3.0 * math.pi) - 4.0 / (15.0 * math.pi) - 4.0 / (35.0 * math.pi),
    8.0 / (3.0 * math.pi) + 32.0 / (15.0 * math.pi) + 72.0 / (35.0 * math.pi),
    -32.0 / (15.0 * math.pi) - 192.0 / (35.0 * math.pi),
    128.0 / (35.0 * math.pi),
)


def passed_along(block, axis, distance):
    devices = range(lax.axis_size(axis))
    route = [((i - distance) % len(devices), i) for i in devices]
    return lax.ppermute(block, axis, route)


def by_axis(shard, axes):
    for axis in axes:
        shard = lax.psum(shard, axis)
    return shard


def in_blocks(shard, dim, count):
    before, after = (shard.shape[:dim], shard.shape[dim + 1 :])
    return jnp.moveaxis(shard.reshape(*before, count, -1, *after), dim, 0)


def sent_and_summed(shard, axis, dim):
    count = lax.axis_size(axis)
    pieces = lax.all_to_all(in_blocks(shard, dim, count), axis, 0, 0, tiled=True)
    return jnp.sum(pieces, axis=0)


def skew_rows(block, width):
    height = block.shape[0]
    length = block.shape[1]
    flattened = jnp.concatenate([block.reshape(-1), jnp.zeros((height,), block.dtype)])
    return flattened.reshape(height, length + 1)[:, :width]


def unskew_rows(band_rows):
    height = band_rows.shape[0]
    width = band_rows.shape[1]
    length = height + width
    padded = jnp.pad(band_rows, ((0, 0), (0, length + 1 - width)))
    return padded.reshape(-1)[: height * length].reshape(height, length)


def on_device(perturbations, probes):
    row_count = lax.axis_size(ROW)
    col_count = lax.axis_size(COL)
    row_index = lax.axis_index(ROW)
    piece_rows = probes.shape[0]
    probe_width = probes.shape[1]
    block_rows = piece_rows * row_count
    state_count = block_rows * col_count
    window_width = state_count // 4
    reach_blocks = col_count // 4
    sub_rows = min(256, block_rows)
    pieces_list = []
    for offset in range(-reach_blocks, reach_blocks + 1):
        if offset == 0:
            pieces_list.append(perturbations)
        else:
            pieces_list.append(passed_along(perturbations, COL, -offset))
    member_window = jnp.concatenate(pieces_list, 1)
    slab_list = []
    for target in range(row_count):
        slab_list.append(
            jnp.concatenate(
                [member_window[:, target * block_rows : (target + 2) * block_rows], perturbations],
                1,
            )
        )
    regrouped = lax.all_to_all(
        jnp.stack(slab_list, 0), ROW, split_axis=0, concat_axis=1, tiled=True
    )[0]
    centered = regrouped - jnp.sum(regrouped, 0) / MEMBERS
    normed = centered / jnp.sqrt(jnp.sum(centered * centered, 0) + epsilon)
    col_panel = normed[:, : 2 * block_rows]
    row_panel = normed[:, 2 * block_rows :]
    offsets = row_index * block_rows + jnp.arange(block_rows, dtype=jnp.int32)
    taper = jnp.maximum(
        jnp.float32(0.0), 1.0 - jnp.abs(offsets - window_width).astype(jnp.float32) / window_width
    )
    band_list = []
    for first_row in range(0, block_rows, sub_rows):
        row_slice = row_panel[:, first_row : first_row + sub_rows]
        col_slice = col_panel[:, first_row : first_row + sub_rows + block_rows]
        gram_block = lax.dot_general(
            row_slice,
            col_slice,
            (((0,), (0,)), ((), ())),
            precision=lax.Precision.HIGHEST,
            preferred_element_type=jnp.float32,
        )
        band_list.append(skew_rows(gram_block, block_rows) * taper)
    localized = jnp.concatenate(band_list, 0)
    scale_norm = by_axis(jnp.sum(localized * localized), ROW_COL) / state_count
    vector = probes
    summed_terms = power_terms[0] * probes
    for power in range(1, STEPS + 1):
        rows_list = []
        for advance_offset in range(-reach_blocks, reach_blocks + 1):
            if advance_offset == 0:
                rows_list.append(vector)
            else:
                rows_list.append(passed_along(vector, COL, -advance_offset))
        probe_window = jnp.concatenate(rows_list, 0)
        target_list = []
        for advance_target in range(row_count):
            target_list.append(
                probe_window[
                    advance_target * piece_rows : (advance_target + 2) * piece_rows
                ].reshape(2, piece_rows, probe_width)
            )
        arrived = lax.all_to_all(
            jnp.stack(target_list, 1), ROW, split_axis=1, concat_axis=1, tiled=True
        )
        window_rows = arrived.reshape(2 * block_rows, probe_width)
        begin_row = jnp.int32(0)
        results = []
        for part_index in range(piece_rows * lax.axis_size(ROW) // sub_rows):
            band_first_row = begin_row + part_index * sub_rows
            band_rows = lax.dynamic_slice_in_dim(localized, band_first_row, sub_rows, 0)
            near_rows = lax.dynamic_slice_in_dim(
                window_rows, band_first_row, sub_rows + block_rows, 0
            )
            results.append(
                jnp.dot(
                    unskew_rows(band_rows),
                    near_rows,
                    precision=lax.Precision.HIGHEST,
                    preferred_element_type=jnp.float32,
                )
            )
        vector = sent_and_summed(jnp.concatenate(results, 0), ROW, 0) / scale_norm
        summed_terms = summed_terms + power_terms[power] * vector
    sampled = jnp.sqrt(scale_norm) * summed_terms
    return (localized, sampled)


def solution(mesh):
    finer = Mesh(mesh.devices.reshape(2, 4, 2, 4, 2), ("row_0", "row_1", "col_0", "col_1", "col_2"))
    placed = (P(ROW, COL), P(COL_ROW, None))
    return jax.shard_map(
        on_device,
        mesh=finer,
        in_specs=placed,
        out_specs=(P(COL, ROW), P(COL_ROW, None)),
        check_vma=False,
    )
```

profile of v0, /device:TPU:32, one launch (start us, length us, event | category | flops | bytes accessed | tf_op | source)
XLA Modules:
  0.0 386.6 jit_solution(12420382299554843199)
XLA Ops:
  0.6 5.5 %collective-permute-start.15 = (f32[128,128]{1,0:T(8,128)}, f32[128,128]{1,0:T(8,128)S(1)}, u32[]{:S(2)}, u32[]{:S(2)}) collective-permute-start(f32[128,128]{1,0:T(8,128)} %param.3), channel_id=1, source_target_pairs={{4,0},{5,1},{6,2},{7,3},{8,4},{9,5},{10,6},{11,7},{12,8},{13,9},{1... | collective-permute-start | bytes 196616 | tf_op jit(solution)/shard_map/ppermute | solution.py:29
  29.7 4.5 %all-to-all-start.1 = ((f32[2,8,128,128]{3,2,0,1:T(8,128)}), f32[2,8,128,128]{3,2,0,1:T(8,128)S(1)}, u32[]{:S(2)}, u32[]{:S(2)}) async-start(f32[2,8,128,128]{3,2,0,1:T(8,128)} %constant_dynamic-update-slice_fusion), calls=%async_computation.1 | async-start | bytes 2097152 | tf_op jit(solution)/shard_map/all_to_all | solution.py:132
  34.2 4.2 %collective-permute-start.5 = (f32[64,1024]{1,0:T(8,128)S(1)}, f32[64,1024]{1,0:T(8,128)S(1)}, u32[]{:S(2)}, u32[]{:S(2)}) collective-permute-start(f32[64,1024]{1,0:T(8,128)S(1)} %copy-done.4), channel_id=1, source_target_pairs={{2,0},{3,1},{4,2},{5,3},{6,4},{7,5},{8,6},{9,7},{10,8},{11,9},{12,... | collective-permute-start | bytes 786440 | tf_op jit(solution)/shard_map/ppermute | solution.py:29
  39.6 3.9 %collective-permute-start.7 = (f32[64,1024]{1,0:T(8,128)S(1)}, f32[64,1024]{1,0:T(8,128)S(1)}, u32[]{:S(2)}, u32[]{:S(2)}) collective-permute-start(f32[64,1024]{1,0:T(8,128)S(1)} %copy-done.4), channel_id=1, source_target_pairs={{4,0},{5,1},{6,2},{7,3},{8,4},{9,5},{10,6},{11,7},{12,8},{13,9},{1... | collective-permute-start | bytes 786440 | tf_op jit(solution)/shard_map/ppermute | solution.py:29
  48.3 4.5 %collective-permute-done.6 = f32[64,1024]{1,0:T(8,128)S(1)} collective-permute-done((f32[64,1024]{1,0:T(8,128)S(1)}, f32[64,1024]{1,0:T(8,128)S(1)}, u32[]{:S(2)}, u32[]{:S(2)}) %collective-permute-start.6) | collective-permute-done | bytes 262176 | tf_op jit(solution)/shard_map/ppermute | solution.py:29
  53.8 4.2 %collective-permute-done.7 = f32[64,1024]{1,0:T(8,128)S(1)} collective-permute-done((f32[64,1024]{1,0:T(8,128)S(1)}, f32[64,1024]{1,0:T(8,128)S(1)}, u32[]{:S(2)}, u32[]{:S(2)}) %collective-permute-start.7) | collective-permute-done | bytes 262176 | tf_op jit(solution)/shard_map/ppermute | solution.py:29
  58.9 5.3 %all-to-all-start = ((f32[8,64,3072]{2,1,0:T(8,128)}), f32[8,64,3072]{2,1,0:T(8,128)}, u32[]{:S(2)}, u32[]{:S(2)}) async-start(f32[8,64,3072]{2,1,0:T(8,128)} %fusion.24), calls=%async_computation | async-start | bytes 12582912 | tf_op jit(solution)/shard_map/all_to_all | solution.py:90
  65.4 66.5 %all-to-all-done = f32[8,64,3072]{2,1,0:T(8,128)} async-done(((f32[8,64,3072]{2,1,0:T(8,128)}), f32[8,64,3072]{2,1,0:T(8,128)}, u32[]{:S(2)}, u32[]{:S(2)}) %all-to-all-start) | async-done | bytes 6291488 | tf_op jit(solution)/shard_map/all_to_all | solution.py:90
  135.0 3.5 multiply_reduce_fusion
  138.5 3.9 %fusion = f32[512,3072]{1,0:T(8,128)S(1)} fusion(f32[8,64,3072]{2,1,0:T(8,128)} %all-to-all-done, f32[3072]{0:T(1024)S(1)} %add_sqrt_fusion, f32[3072]{0:T(1024)S(1)} %broadcast_multiply_fusion), kind=kLoop, calls=%fused_computation.1 | loop fusion | flops 3145728 | bytes 12607488 | tf_op jit(solution)/shard_map/div | solution.py:94
  144.8 3.4 fusion.5
  168.8 4.3 %slice_multiply_fusion.3 = (f32[256,1024]{1,0:T(8,128)}, f32[256,1024]{1,0:T(8,128)}, f32[256,1024]{1,0:T(8,128)S(1)}, f32[256,1024]{1,0:T(8,128)S(1)}) fusion(f32[256,1281]{1,0:T(8,128)} %reshape.113, f32[1024]{0:T(1024)S(1)} %subtract_maximum_fusion, f32[256,1281]{1,0:T(8,128)} %reshape.115, f32[256,1281]{1,0:T(8,128)} %reshape.117, f32[256,1281]{1,0:T(8,128)} %reshape.119), kind=kLoop, calls=%fused_computation.24 | loop fusion | flops 1048576 | bytes 8392704 | tf_op jit(solution)/shard_map/mul | solution.py:112
  216.7 3.6 all-to-all-start.2
  220.3 5.9 %multiply_reduce_fusion.1 = (f32[]{:T(128)}, f32[1024,1024]{1,0:T(8,128)}) fusion(f32[256,1024]{1,0:T(8,128)} %copy-done.9, f32[256,1024]{1,0:T(8,128)} %copy-done.8, f32[256,1024]{1,0:T(8,128)} %get-tuple-element.29, f32[256,1024]{1,0:T(8,128)} %get-tuple-element.28), kind=kLoop, calls=%fused_computation.4 | loop fusion | flops 5242879 | bytes 8388612 | tf_op jit(solution)/shard_map/reduce_sum | solution.py:114
  226.1 5.5 %psum.35 = f32[]{:T(128)} all-reduce(f32[]{:T(128)} %get-tuple-element.2), channel_id=1, replica_groups=mesh['row_0'=2,'row_1'=4,'col_0'=2,'col_1'=4,'col_2'=2] {'row_0'}, use_global_device_ids=true, to_apply=%region_3.0 | all-reduce | flops 1 | bytes 8 | tf_op jit(solution)/shard_map/psum | solution.py:34
  231.7 11.6 %psum.36 = f32[]{:T(128)} all-reduce(f32[]{:T(128)} %psum.35), channel_id=1, replica_groups=mesh['row_0'=2,'row_1'=4,'col_0'=2,'col_1'=4,'col_2'=2] {'row_1'}, use_global_device_ids=true, to_apply=%region_4.0 | all-reduce | flops 1 | bytes 8 | tf_op jit(solution)/shard_map/psum | solution.py:34
  243.3 7.1 %psum.37 = f32[]{:T(128)} all-reduce(f32[]{:T(128)} %psum.36), channel_id=1, replica_groups=mesh['row_0'=2,'row_1'=4,'col_0'=2,'col_1'=4,'col_2'=2] {'col_0'}, use_global_device_ids=true, to_apply=%region_5.0 | all-reduce | flops 1 | bytes 8 | tf_op jit(solution)/shard_map/psum | solution.py:34
  250.3 19.2 %psum.38 = f32[]{:T(128)} all-reduce(f32[]{:T(128)} %psum.37), channel_id=1, replica_groups=mesh['row_0'=2,'row_1'=4,'col_0'=2,'col_1'=4,'col_2'=2] {'col_1'}, use_global_device_ids=true, to_apply=%region_6.0 | all-reduce | flops 1 | bytes 8 | tf_op jit(solution)/shard_map/psum | solution.py:34
  289.5 3.6 collective-permute-done.16
  293.4 18.6 %all_to_all.39 = f32[2,8,128,128]{3,2,0,1:T(8,128)S(1)} all-to-all(f32[2,8,128,128]{3,2,0,1:T(8,128)S(1)} %constant_dynamic-update-slice_fusion.8), channel_id=1, replica_groups=mesh['row_0'=2,'row_1'=4,'col_0'=2,'col_1'=4,'col_2'=2] {'row_0','row_1'}, dimensions={1} | all-to-all | bytes 2097152 | tf_op jit(solution)/shard_map/all_to_all | solution.py:132
  317.2 12.2 %all_to_all.40 = f32[8,128,128]{2,1,0:T(8,128)S(1)} all-to-all(f32[8,128,128]{2,1,0:T(8,128)S(1)} %bitcast.91), channel_id=1, replica_groups=mesh['row_0'=2,'row_1'=4,'col_0'=2,'col_1'=4,'col_2'=2] {'row_0','row_1'}, dimensions={0} | all-to-all | bytes 1048576 | tf_op jit(solution)/shard_map/all_to_all | solution.py:45
  347.2 19.2 %all_to_all.41 = f32[2,8,128,128]{3,2,0,1:T(8,128)S(1)} all-to-all(f32[2,8,128,128]{3,2,0,1:T(8,128)S(1)} %constant_dynamic-update-slice_fusion.16), channel_id=1, replica_groups=mesh['row_0'=2,'row_1'=4,'col_0'=2,'col_1'=4,'col_2'=2] {'row_0','row_1'}, dimensions={1} | all-to-all | bytes 2097152 | tf_op jit(solution)/shard_map/all_to_all | solution.py:132
  372.4 3.5 all-to-all-start.6
  376.0 9.4 %all-to-all-done.6 = f32[8,128,128]{2,1,0:T(8,128)S(1)} async-done(((f32[8,128,128]{2,1,0:T(8,128)}), f32[8,128,128]{2,1,0:T(8,128)S(1)}, u32[]{:S(2)}, u32[]{:S(2)}) %all-to-all-start.6) | async-done | bytes 524320 | tf_op jit(solution)/shard_map/all_to_all | solution.py:45
  (177 shorter events, 150.9 us)
Async XLA Ops:
  6.1 8.6 %collective-permute-start.13 = (f32[128,128]{1,0:T(8,128)}, f32[128,128]{1,0:T(8,128)S(1)}, u32[]{:S(2)}, u32[]{:S(2)}) collective-permute-start(f32[128,128]{1,0:T(8,128)} %param.3), channel_id=1, source_target_pairs={{2,0},{3,1},{4,2},{5,3},{6,4},{7,5},{8,6},{9,7},{10,8},{11,9},{12,... | collective-permute-start | bytes 196616 | tf_op jit(solution)/shard_map/ppermute | solution.py:29
  7.2 9.7 %collective-permute-start.12 = (f32[128,128]{1,0:T(8,128)}, f32[128,128]{1,0:T(8,128)S(1)}, u32[]{:S(2)}, u32[]{:S(2)}) collective-permute-start(f32[128,128]{1,0:T(8,128)} %param.3), channel_id=1, source_target_pairs={{1,0},{2,1},{3,2},{4,3},{5,4},{6,5},{7,6},{8,7},{9,8},{10,9},{11,1... | collective-permute-start | bytes 196616 | tf_op jit(solution)/shard_map/ppermute | solution.py:29
  7.6 10.8 %collective-permute-start.11 = (f32[128,128]{1,0:T(8,128)}, f32[128,128]{1,0:T(8,128)S(1)}, u32[]{:S(2)}, u32[]{:S(2)}) collective-permute-start(f32[128,128]{1,0:T(8,128)} %param.3), channel_id=1, source_target_pairs={{15,0},{0,1},{1,2},{2,3},{3,4},{4,5},{5,6},{6,7},{7,8},{8,9},{9,10... | collective-permute-start | bytes 196616 | tf_op jit(solution)/shard_map/ppermute | solution.py:29
  8.4 11.7 %collective-permute-start.10 = (f32[128,128]{1,0:T(8,128)}, f32[128,128]{1,0:T(8,128)S(1)}, u32[]{:S(2)}, u32[]{:S(2)}) collective-permute-start(f32[128,128]{1,0:T(8,128)} %param.3), channel_id=1, source_target_pairs={{14,0},{15,1},{0,2},{1,3},{2,4},{3,5},{4,6},{5,7},{6,8},{7,9},{8,1... | collective-permute-start | bytes 196616 | tf_op jit(solution)/shard_map/ppermute | solution.py:29
  11.6 10.1 %collective-permute-start.9 = (f32[128,128]{1,0:T(8,128)}, f32[128,128]{1,0:T(8,128)S(1)}, u32[]{:S(2)}, u32[]{:S(2)}) collective-permute-start(f32[128,128]{1,0:T(8,128)} %param.3), channel_id=1, source_target_pairs={{13,0},{14,1},{15,2},{0,3},{1,4},{2,5},{3,6},{4,7},{5,8},{6,9},{7,... | collective-permute-start | bytes 196616 | tf_op jit(solution)/shard_map/ppermute | solution.py:29
  14.7 8.5 %collective-permute-start.8 = (f32[128,128]{1,0:T(8,128)}, f32[128,128]{1,0:T(8,128)S(1)}, u32[]{:S(2)}, u32[]{:S(2)}) collective-permute-start(f32[128,128]{1,0:T(8,128)} %param.3), channel_id=1, source_target_pairs={{12,0},{13,1},{14,2},{15,3},{0,4},{1,5},{2,6},{3,7},{4,8},{5,9},{6... | collective-permute-start | bytes 196616 | tf_op jit(solution)/shard_map/ppermute | solution.py:29
  16.9 17.3 %collective-permute-start.1 = (f32[64,1024]{1,0:T(8,128)}, f32[64,1024]{1,0:T(8,128)S(1)}, u32[]{:S(2)}, u32[]{:S(2)}) collective-permute-start(f32[64,1024]{1,0:T(8,128)} %param.2), channel_id=1, source_target_pairs={{13,0},{14,1},{15,2},{0,3},{1,4},{2,5},{3,6},{4,7},{5,8},{6,9},{7,... | collective-permute-start | bytes 786440 | tf_op jit(solution)/shard_map/ppermute | solution.py:29
  18.4 20.0 %collective-permute-start = (f32[64,1024]{1,0:T(8,128)}, f32[64,1024]{1,0:T(8,128)S(1)}, u32[]{:S(2)}, u32[]{:S(2)}) collective-permute-start(f32[64,1024]{1,0:T(8,128)} %param.2), channel_id=1, source_target_pairs={{12,0},{13,1},{14,2},{15,3},{0,4},{1,5},{2,6},{3,7},{4,8},{5,9},{6... | collective-permute-start | bytes 786440 | tf_op jit(solution)/shard_map/ppermute | solution.py:29
  20.1 19.5 %collective-permute-start.2 = (f32[64,1024]{1,0:T(8,128)}, f32[64,1024]{1,0:T(8,128)S(1)}, u32[]{:S(2)}, u32[]{:S(2)}) collective-permute-start(f32[64,1024]{1,0:T(8,128)} %param.2), channel_id=1, source_target_pairs={{14,0},{15,1},{0,2},{1,3},{2,4},{3,5},{4,6},{5,7},{6,8},{7,9},{8,1... | collective-permute-start | bytes 786440 | tf_op jit(solution)/shard_map/ppermute | solution.py:29
  21.6 22.8 %collective-permute-start.3 = (f32[64,1024]{1,0:T(8,128)}, f32[64,1024]{1,0:T(8,128)S(1)}, u32[]{:S(2)}, u32[]{:S(2)}) collective-permute-start(f32[64,1024]{1,0:T(8,128)} %param.2), channel_id=1, source_target_pairs={{15,0},{0,1},{1,2},{2,3},{3,4},{4,5},{5,6},{6,7},{7,8},{8,9},{9,10... | collective-permute-start | bytes 786440 | tf_op jit(solution)/shard_map/ppermute | solution.py:29
  23.2 23.2 %collective-permute-start.4 = (f32[64,1024]{1,0:T(8,128)}, f32[64,1024]{1,0:T(8,128)S(1)}, u32[]{:S(2)}, u32[]{:S(2)}) collective-permute-start(f32[64,1024]{1,0:T(8,128)} %param.2), channel_id=1, source_target_pairs={{1,0},{2,1},{3,2},{4,3},{5,4},{6,5},{7,6},{8,7},{9,8},{10,9},{11,1... | collective-permute-start | bytes 786440 | tf_op jit(solution)/shard_map/ppermute | solution.py:29
  29.7 29.2 %all-to-all-start.1 = ((f32[2,8,128,128]{3,2,0,1:T(8,128)}), f32[2,8,128,128]{3,2,0,1:T(8,128)S(1)}, u32[]{:S(2)}, u32[]{:S(2)}) async-start(f32[2,8,128,128]{3,2,0,1:T(8,128)} %constant_dynamic-update-slice_fusion), calls=%async_computation.1 | async-start | bytes 2097152 | tf_op jit(solution)/shard_map/all_to_all | solution.py:132
  34.2 13.2 %collective-permute-start.5 = (f32[64,1024]{1,0:T(8,128)S(1)}, f32[64,1024]{1,0:T(8,128)S(1)}, u32[]{:S(2)}, u32[]{:S(2)}) collective-permute-start(f32[64,1024]{1,0:T(8,128)S(1)} %copy-done.4), channel_id=1, source_target_pairs={{2,0},{3,1},{4,2},{5,3},{6,4},{7,5},{8,6},{9,7},{10,8},{11,9},{12,... | collective-permute-start | bytes 786440 | tf_op jit(solution)/shard_map/ppermute | solution.py:29
  38.5 14.4 %collective-permute-start.6 = (f32[64,1024]{1,0:T(8,128)S(1)}, f32[64,1024]{1,0:T(8,128)S(1)}, u32[]{:S(2)}, u32[]{:S(2)}) collective-permute-start(f32[64,1024]{1,0:T(8,128)S(1)} %copy-done.4), channel_id=1, source_target_pairs={{3,0},{4,1},{5,2},{6,3},{7,4},{8,5},{9,6},{10,7},{11,8},{12,9},{13... | collective-permute-start | bytes 786440 | tf_op jit(solution)/shard_map/ppermute | solution.py:29
  39.6 18.4 %collective-permute-start.7 = (f32[64,1024]{1,0:T(8,128)S(1)}, f32[64,1024]{1,0:T(8,128)S(1)}, u32[]{:S(2)}, u32[]{:S(2)}) collective-permute-start(f32[64,1024]{1,0:T(8,128)S(1)} %copy-done.4), channel_id=1, source_target_pairs={{4,0},{5,1},{6,2},{7,3},{8,4},{9,5},{10,6},{11,7},{12,8},{13,9},{1... | collective-permute-start | bytes 786440 | tf_op jit(solution)/shard_map/ppermute | solution.py:29
  58.9 72.9 %all-to-all-start = ((f32[8,64,3072]{2,1,0:T(8,128)}), f32[8,64,3072]{2,1,0:T(8,128)}, u32[]{:S(2)}, u32[]{:S(2)}) async-start(f32[8,64,3072]{2,1,0:T(8,128)} %fusion.24), calls=%async_computation | async-start | bytes 12582912 | tf_op jit(solution)/shard_map/all_to_all | solution.py:90
  216.7 56.6 %all-to-all-start.2 = ((f32[8,128,128]{2,1,0:T(8,128)}), f32[8,128,128]{2,1,0:T(8,128)S(1)}, u32[]{:S(2)}, u32[]{:S(2)}) async-start(f32[8,128,128]{2,1,0:T(8,128)} %bitcast.90), calls=%async_computation.2 | async-start | bytes 1048576 | tf_op jit(solution)/shard_map/all_to_all | solution.py:45
  278.1 8.7 %collective-permute-start.20 = (f32[128,128]{1,0:T(8,128)S(1)}, f32[128,128]{1,0:T(8,128)S(1)}, u32[]{:S(2)}, u32[]{:S(2)}) collective-permute-start(f32[128,128]{1,0:T(8,128)S(1)} %broadcast_divide_fusion.1), channel_id=1, source_target_pairs={{1,0},{2,1},{3,2},{4,3},{5,4},{6,5},{7,6},{8,7},{9,8},{10,9},{11,1... | collective-permute-start | bytes 196616 | tf_op jit(solution)/shard_map/ppermute | solution.py:29
  281.3 8.2 %collective-permute-start.17 = (f32[128,128]{1,0:T(8,128)S(1)}, f32[128,128]{1,0:T(8,128)S(1)}, u32[]{:S(2)}, u32[]{:S(2)}) collective-permute-start(f32[128,128]{1,0:T(8,128)S(1)} %broadcast_divide_fusion.1), channel_id=1, source_target_pairs={{13,0},{14,1},{15,2},{0,3},{1,4},{2,5},{3,6},{4,7},{5,8},{6,9},{7,... | collective-permute-start | bytes 196616 | tf_op jit(solution)/shard_map/ppermute | solution.py:29
  284.6 8.5 %collective-permute-start.16 = (f32[128,128]{1,0:T(8,128)S(1)}, f32[128,128]{1,0:T(8,128)S(1)}, u32[]{:S(2)}, u32[]{:S(2)}) collective-permute-start(f32[128,128]{1,0:T(8,128)S(1)} %broadcast_divide_fusion.1), channel_id=1, source_target_pairs={{12,0},{13,1},{14,2},{15,3},{0,4},{1,5},{2,6},{3,7},{4,8},{5,9},{6... | collective-permute-start | bytes 196616 | tf_op jit(solution)/shard_map/ppermute | solution.py:29
  330.3 8.5 %collective-permute-start.29 = (f32[128,128]{1,0:T(8,128)S(1)}, f32[128,128]{1,0:T(8,128)S(1)}, u32[]{:S(2)}, u32[]{:S(2)}) collective-permute-start(f32[128,128]{1,0:T(8,128)S(1)} %broadcast_divide_fusion), channel_id=1, source_target_pairs={{2,0},{3,1},{4,2},{5,3},{6,4},{7,5},{8,6},{9,7},{10,8},{11,9},{12,... | collective-permute-start | bytes 196616 | tf_op jit(solution)/shard_map/ppermute | solution.py:29
  332.3 9.3 %collective-permute-start.28 = (f32[128,128]{1,0:T(8,128)S(1)}, f32[128,128]{1,0:T(8,128)S(1)}, u32[]{:S(2)}, u32[]{:S(2)}) collective-permute-start(f32[128,128]{1,0:T(8,128)S(1)} %broadcast_divide_fusion), channel_id=1, source_target_pairs={{1,0},{2,1},{3,2},{4,3},{5,4},{6,5},{7,6},{8,7},{9,8},{10,9},{11,1... | collective-permute-start | bytes 196616 | tf_op jit(solution)/shard_map/ppermute | solution.py:29
  338.7 8.2 %collective-permute-start.24 = (f32[128,128]{1,0:T(8,128)S(1)}, f32[128,128]{1,0:T(8,128)S(1)}, u32[]{:S(2)}, u32[]{:S(2)}) collective-permute-start(f32[128,128]{1,0:T(8,128)S(1)} %broadcast_divide_fusion), channel_id=1, source_target_pairs={{12,0},{13,1},{14,2},{15,3},{0,4},{1,5},{2,6},{3,7},{4,8},{5,9},{6... | collective-permute-start | bytes 196616 | tf_op jit(solution)/shard_map/ppermute | solution.py:29
  372.4 13.0 %all-to-all-start.6 = ((f32[8,128,128]{2,1,0:T(8,128)}), f32[8,128,128]{2,1,0:T(8,128)S(1)}, u32[]{:S(2)}, u32[]{:S(2)}) async-start(f32[8,128,128]{2,1,0:T(8,128)} %bitcast.38), calls=%async_computation.6 | async-start | bytes 1048576 | tf_op jit(solution)/shard_map/all_to_all | solution.py:45
  (23 other events, 124.7 us)
where the time goes:
time: 393 us; the launch traced here: 387 us
  waiting for transfers between devices  99.6 us (25%)
  blocking collectives  96.5 us (25%)
  starting transfers between devices  70.3 us (18%)
  local copies, waits for them, and re-layouts  54.5 us (14%)
  other arithmetic  32 us (8%)
  matrix products  31.3 us (8%)
    all_to_all x1, waiting for transfers between devices, on_device(): lax.all_to_all(jnp.stack(slab_list, 0), ROW, split_axis=0, concat_axis=1,...  66.5 us
    ppermute x32, starting transfers between devices, passed_along(): return lax.ppermute(block, axis, route)  53.4 us
    psum x5, blocking collectives, by_axis(): shard = lax.psum(shard, axis)  46.5 us
    all_to_all x2, blocking collectives, on_device(): lax.all_to_all(jnp.stack(target_list, 1), ROW, split_axis=1, concat_axis=...  37.9 us
    ppermute x32, waiting for transfers between devices, passed_along(): return lax.ppermute(block, axis, route)  23.6 us
    reshape x8, local copies, waits for them, and re-layouts, unskew_rows(): return padded.reshape(-1)[:height * length].reshape(height, length)  20.2 us
    dot_general x12, matrix products, on_device(): jnp.dot(unskew_rows(band_rows), near_rows, precision=lax.Precision.HIGHES...  18.6 us
    dot_general x4, matrix products, on_device(): lax.dot_general(row_slice, col_slice, (((0,), (0,)), ((), ())), precision...  12.7 us
  transfers between devices with their start and end apart: 36, of which 12 were waited for; matrix products, arithmetic and copies ran while one was open for 5% of the time, Pallas kernels for 0%

commit v1 on v0

v1 whole, which is shorter than its diff:
```python
import functools
import math

import jax
import jax.numpy as jnp
from jax import lax
from jax.experimental import pallas as pl
from jax.experimental.pallas import tpu as pltpu
from jax.sharding import PartitionSpec as P

MEMBERS = 512
STATES = 16384
WINDOW = 4096
ROWS = 8
COLS = 16
BLOCK = 1024
PIECE = 128
SUB = 256
SPAN = SUB + BLOCK
STEPS = 3
MESH = pl.DeviceIdType.MESH
VMEM_LIMIT = 58 * 2**20

epsilon = 1e-06
power_terms = (
    2.0 / math.pi - 4.0 / (3.0 * math.pi) - 4.0 / (15.0 * math.pi) - 4.0 / (35.0 * math.pi),
    8.0 / (3.0 * math.pi) + 32.0 / (15.0 * math.pi) + 72.0 / (35.0 * math.pi),
    -32.0 / (15.0 * math.pi) - 192.0 / (35.0 * math.pi),
    128.0 / (35.0 * math.pi),
)


def here():
    return lax.axis_index("row"), lax.axis_index("col")


def at(row, col):
    return {"row": row, "col": col}


def reached(r, c):
    found = []
    for panel in range(2):
        for row in range(ROWS):
            col = lax.rem(c + (4 - panel) - row + 2 * COLS, COLS)
            own = (r == row) if row == 4 - panel else None
            found.append((row, col, panel, own))
    return found


def unless(own, step):
    if own is None:
        step()
    else:
        pl.when(jnp.logical_not(own))(step)


def copied(src, dst, send, recv, row, col):
    return pltpu.make_async_remote_copy(
        src_ref=src, dst_ref=dst, send_sem=send, recv_sem=recv,
        device_id=at(row, col), device_id_type=MESH,
    )


def gather_kernel(x_ref, out_ref, send_row, send_need, recv):
    r, c = here()
    barrier = pltpu.get_barrier_semaphore()
    for shift in range(1, ROWS):
        pl.semaphore_signal(barrier, inc=1, device_id=at(lax.rem(r + shift, ROWS), c), device_id_type=MESH)
    for panel in range(2):
        block = lax.rem(c + r - 4 + panel + COLS, COLS)
        for row in range(ROWS):
            own = None
            if row == 4 - panel:
                own = r == row

            def greet(row=row, block=block):
                pl.semaphore_signal(barrier, inc=1, device_id=at(row, block), device_id_type=MESH)

            unless(own, greet)
    pl.semaphore_wait(barrier, 7 + 16 - jnp.where((r == 3) | (r == 4), 1, 0))

    for row, col, panel, own in reached(r, c):
        def go(row=row, col=col, panel=panel):
            copied(x_ref, out_ref.at[1 + panel, r], send_need.at[panel, row], recv.at[1 + panel, r], row, col).start()

        unless(own, go)
        if own is not None:
            @pl.when(own)
            def _(panel=panel):
                pltpu.make_async_copy(x_ref, out_ref.at[1 + panel, r], recv.at[1 + panel, r]).start()
    for shift in range(1, ROWS):
        copied(x_ref, out_ref.at[0, r], send_row.at[shift], recv.at[0, r], lax.rem(r + shift, ROWS), c).start()
    pltpu.make_async_copy(x_ref, out_ref.at[0, r], recv.at[0, r]).start()

    for row, col, panel, own in reached(r, c):
        def done(row=row, col=col, panel=panel):
            copied(x_ref, out_ref.at[1 + panel, r], send_need.at[panel, row], recv.at[1 + panel, r], row, col).wait_send()

        unless(own, done)
    for shift in range(1, ROWS):
        copied(x_ref, out_ref.at[0, r], send_row.at[shift], recv.at[0, r], lax.rem(r + shift, ROWS), c).wait_send()
    for panel in range(3):
        for row in range(ROWS):
            pltpu.make_async_copy(x_ref, out_ref.at[panel, row], recv.at[panel, row]).wait()


def gathered(block):
    return pl.pallas_call(
        gather_kernel,
        name="gather_members",
        out_shape=jax.ShapeDtypeStruct((3, ROWS, MEMBERS // ROWS, BLOCK), jnp.float32),
        in_specs=[pl.BlockSpec(memory_space=pl.ANY)],
        out_specs=pl.BlockSpec(memory_space=pl.ANY),
        scratch_shapes=[
            pltpu.SemaphoreType.DMA((ROWS,)),
            pltpu.SemaphoreType.DMA((2, ROWS)),
            pltpu.SemaphoreType.DMA((3, ROWS)),
        ],
        compiler_params=pltpu.CompilerParams(collective_id=1, has_side_effects=True),
    )(block)


def parted(values):
    high = values.astype(jnp.bfloat16)
    low = (values - high.astype(jnp.float32)).astype(jnp.bfloat16)
    return high, low


def dotted(a, b, dims):
    return lax.dot_general(a, b, (dims, ((), ())), preferred_element_type=jnp.float32)


def skewed(rows, shift):
    sub = lax.broadcasted_iota(jnp.int32, rows.shape, 0)
    if shift:
        rows = pltpu.roll(rows, SPAN - shift, 1)
    for bit in (1, 2, 4):
        rows = jnp.where((sub & bit) != 0, pltpu.roll(rows, SPAN - bit, 1), rows)
    return rows[:, :BLOCK]


def band_kernel(x_ref, local_ref, high_ref, low_ref, square_ref, xh, xl):
    r, _ = here()
    for panel in range(3):
        for first in range(0, BLOCK, SUB):
            values = x_ref[panel, :, first : first + SUB]
            centered = values - jnp.sum(values, 0, keepdims=True) / MEMBERS
            spread = jnp.sqrt(jnp.sum(centered * centered, 0, keepdims=True) + epsilon)
            high, low = parted(centered / spread)
            lo_at = (panel - 1) * BLOCK + first if panel else 2 * BLOCK + first
            xh[:, lo_at : lo_at + SUB] = high
            xl[:, lo_at : lo_at + SUB] = low
    squares = jnp.zeros((8, 128), jnp.float32)
    gap = lax.broadcasted_iota(jnp.int32, (SUB, SPAN), 1) - lax.broadcasted_iota(jnp.int32, (SUB, SPAN), 0)
    taper = jnp.maximum(0.0, 1.0 - jnp.abs(gap + (r * BLOCK - WINDOW)).astype(jnp.float32) / WINDOW)
    taper = jnp.where((gap >= 0) & (gap < BLOCK), taper, 0.0)
    for tile in range(BLOCK // SUB):
        first = tile * SUB
        rows_h = xh[:, 2 * BLOCK + first : 2 * BLOCK + first + SUB]
        rows_l = xl[:, 2 * BLOCK + first : 2 * BLOCK + first + SUB]
        cols_h = xh[:, first : first + SPAN]
        cols_l = xl[:, first : first + SPAN]
        over = ((0,), (0,))
        gram = dotted(rows_h, cols_h, over) + (dotted(rows_h, cols_l, over) + dotted(rows_l, cols_h, over))
        band = gram * taper
        high, low = parted(band)
        high_ref[tile] = high
        low_ref[tile] = low
        squares = squares + jnp.sum((band * band).reshape(SUB // 8, 8, SPAN // 128, 128), (0, 2))
        for group in range(0, SUB, 8):
            local_ref[first + group : first + group + 8, :] = skewed(band[group : group + 8, :], group)
    square_ref[...] = squares


def banded(panels):
    return pl.pallas_call(
        band_kernel,
        name="band",
        out_shape=(
            jax.ShapeDtypeStruct((BLOCK, BLOCK), jnp.float32),
            jax.ShapeDtypeStruct((BLOCK // SUB, SUB, SPAN), jnp.bfloat16),
            jax.ShapeDtypeStruct((BLOCK // SUB, SUB, SPAN), jnp.bfloat16),
            jax.ShapeDtypeStruct((8, 128), jnp.float32),
        ),
        in_specs=[pl.BlockSpec(memory_space=pltpu.VMEM)],
        out_specs=[pl.BlockSpec(memory_space=pltpu.VMEM)] * 4,
        scratch_shapes=[
            pltpu.VMEM((MEMBERS, 3 * BLOCK), jnp.bfloat16),
            pltpu.VMEM((MEMBERS, 3 * BLOCK), jnp.bfloat16),
        ],
        compiler_params=pltpu.CompilerParams(vmem_limit_bytes=VMEM_LIMIT),
    )(panels)


def product_kernel(
    w_ref, high_ref, low_ref, square_ref, out_ref,
    iterate, window, wide, parts, sums, row_squares, col_squares, row_total,
    send_w, recv_w, send_y, recv_y, send_r, recv_r, send_c, recv_c,
):
    r, c = here()
    barrier = pltpu.get_barrier_semaphore()
    for shift in range(1, ROWS):
        pl.semaphore_signal(barrier, inc=1, device_id=at(lax.rem(r + shift, ROWS), c), device_id_type=MESH)
    for shift in range(1, COLS):
        pl.semaphore_signal(barrier, inc=1, device_id=at(r, lax.rem(c + shift, COLS)), device_id_type=MESH)
    for panel in range(2):
        block = lax.rem(c + r - 4 + panel + COLS, COLS)
        for row in range(ROWS):
            own = (r == row) if row == 4 - panel else None

            def greet(row=row, block=block):
                pl.semaphore_signal(barrier, inc=1, device_id=at(row, block), device_id_type=MESH)

            unless(own, greet)
    pl.semaphore_wait(barrier, 7 + 15 + 16 - jnp.where((r == 3) | (r == 4), 1, 0))

    def send_iterate(step, source):
        for row, col, panel, own in reached(r, c):
            def go(row=row, col=col, panel=panel):
                copied(source, window.at[step, panel, r], send_w.at[step, panel, row], recv_w.at[step, panel, r], row, col).start()

            unless(own, go)
            if own is not None:
                @pl.when(own)
                def _(panel=panel):
                    pltpu.make_async_copy(source, window.at[step, panel, r], recv_w.at[step, panel, r]).start()

    for shift in range(1, ROWS):
        copied(square_ref, row_squares.at[r], send_r.at[shift], recv_r.at[r], lax.rem(r + shift, ROWS), c).start()
    pltpu.make_async_copy(square_ref, row_squares.at[r], recv_r.at[r]).start()
    send_iterate(0, w_ref)
    for row in range(ROWS):
        pltpu.make_async_copy(square_ref, row_squares.at[row], recv_r.at[row]).wait()
    row_total[...] = jnp.sum(row_squares[...], 0)
    for shift in range(1, COLS):
        copied(row_total, col_squares.at[c], send_c.at[shift], recv_c.at[c], r, lax.rem(c + shift, COLS)).start()
    pltpu.make_async_copy(row_total, col_squares.at[c], recv_c.at[c]).start()

    total = None
    summed = power_terms[0] * w_ref[...]
    for step in range(STEPS):
        for panel in range(2):
            for row in range(ROWS):
                pltpu.make_async_copy(w_ref, window.at[step, panel, row], recv_w.at[step, panel, row]).wait()
                high, low = parted(window[step, panel, row])
                first = (panel * ROWS + row) * PIECE
                wide[first : first + PIECE, :PIECE] = high
                wide[first : first + PIECE, PIECE:] = low
        for tile in range(BLOCK // SUB):
            first = tile * SUB
            over = ((1,), (0,))
            both = dotted(high_ref[tile], wide[first : first + SPAN, :], over)
            rest = dotted(low_ref[tile], wide[first : first + SPAN, :PIECE], over)
            parts[step, first : first + SUB, :] = both[:, :PIECE] + (both[:, PIECE:] + rest)
            for row in range(first // PIECE, (first + SUB) // PIECE):
                def go(row=row):
                    copied(
                        parts.at[step, row * PIECE : (row + 1) * PIECE], sums.at[step, r],
                        send_y.at[step, row], recv_y.at[step, r], row, c,
                    ).start()

                unless(r == row, go)
        if step == 0:
            for col in range(COLS):
                pltpu.make_async_copy(row_total, col_squares.at[col], recv_c.at[col]).wait()
            total = jnp.sum(jnp.sum(col_squares[...], 0), keepdims=True) / STATES
        vector = parts[step, pl.ds(pl.multiple_of(r * PIECE, PIECE), PIECE), :]
        for row in range(ROWS):
            def landed(row=row):
                pltpu.make_async_copy(w_ref, sums.at[step, row], recv_y.at[step, row]).wait()

            unless(r == row, landed)
            vector = vector + jnp.where(r == row, 0.0, sums[step, row])
        vector = vector / total
        summed = summed + power_terms[step + 1] * vector
        if step < STEPS - 1:
            iterate[step] = vector
            send_iterate(step + 1, iterate.at[step])
    out_ref[...] = jnp.sqrt(total) * summed

    for shift in range(1, ROWS):
        copied(square_ref, row_squares.at[r], send_r.at[shift], recv_r.at[r], lax.rem(r + shift, ROWS), c).wait_send()
    for shift in range(1, COLS):
        copied(row_total, col_squares.at[c], send_c.at[shift], recv_c.at[c], r, lax.rem(c + shift, COLS)).wait_send()
    for step in range(STEPS):
        for row, col, panel, own in reached(r, c):
            def sent(row=row, col=col, panel=panel):
                copied(w_ref, window.at[step, panel, r], send_w.at[step, panel, row], recv_w.at[step, panel, r], row, col).wait_send()

            unless(own, sent)
        for row in range(ROWS):
            def gone(row=row):
                copied(w_ref, sums.at[step, r], send_y.at[step, row], recv_y.at[step, r], row, c).wait_send()

            unless(r == row, gone)


def sampler(probes, high, low, squares):
    return pl.pallas_call(
        product_kernel,
        name="products",
        out_shape=jax.ShapeDtypeStruct((PIECE, PIECE), jnp.float32),
        in_specs=[pl.BlockSpec(memory_space=pltpu.VMEM)] * 4,
        out_specs=pl.BlockSpec(memory_space=pltpu.VMEM),
        scratch_shapes=[
            pltpu.VMEM((STEPS - 1, PIECE, PIECE), jnp.float32),
            pltpu.VMEM((STEPS, 2, ROWS, PIECE, PIECE), jnp.float32),
            pltpu.VMEM((2 * BLOCK, 2 * PIECE), jnp.bfloat16),
            pltpu.VMEM((STEPS, BLOCK, PIECE), jnp.float32),
            pltpu.VMEM((STEPS, ROWS, PIECE, PIECE), jnp.float32),
            pltpu.VMEM((ROWS, 8, 128), jnp.float32),
            pltpu.VMEM((COLS, 8, 128), jnp.float32),
            pltpu.VMEM((8, 128), jnp.float32),
            pltpu.SemaphoreType.DMA((STEPS, 2, ROWS)),
            pltpu.SemaphoreType.DMA((STEPS, 2, ROWS)),
            pltpu.SemaphoreType.DMA((STEPS, ROWS)),
            pltpu.SemaphoreType.DMA((STEPS, ROWS)),
            pltpu.SemaphoreType.DMA((ROWS,)),
            pltpu.SemaphoreType.DMA((ROWS,)),
            pltpu.SemaphoreType.DMA((COLS,)),
            pltpu.SemaphoreType.DMA((COLS,)),
        ],
        compiler_params=pltpu.CompilerParams(
            collective_id=2, has_side_effects=True, vmem_limit_bytes=VMEM_LIMIT
        ),
    )(probes, high, low, squares)


def on_device(perturbations, probes):
    panels = gathered(perturbations).reshape(3, MEMBERS, BLOCK)
    localized, high, low, squares = banded(panels)
    return localized, sampler(probes, high, low, squares)


def solution(mesh):
    return jax.shard_map(
        on_device,
        mesh=mesh,
        in_specs=(P("row", "col"), P(("col", "row"), None)),
        out_specs=(P("col", "row"), P(("col", "row"), None)),
        check_vma=False,
    )
```

time: 393 us -> 313 us (0.80)
  the two profiles are of different devices: /device:TPU:32 before, /device:TPU:26 now
where the time goes in v1:
time: 313 us; the launch traced here: 307 us
  Pallas kernels  305 us (97%)
    pallas_call x1, Pallas kernels, gathered(): pl.pallas_call(gather_kernel, name='gather_members', out_shape=jax.ShapeD...  146 us
    pallas_call x1, Pallas kernels, sampler(): pl.pallas_call(product_kernel, name='products', out_shape=jax.ShapeDtypeS...  137 us
    pallas_call x1, Pallas kernels, banded(): pl.pallas_call(band_kernel, name='band', out_shape=(jax.ShapeDtypeStruct(...  21.9 us

profile of v1, /device:TPU:26, one launch (start us, length us, event | category | flops | bytes accessed | tf_op | source)
XLA Modules:
  0.0 307.0 jit_solution(6227523000330226652)
XLA Ops:
  0.6 146.0 %gather_members.1 = f32[3,8,64,1024]{3,2,1,0:T(8,128)} custom-call(f32[64,1024]{1,0:T(8,128)} %x_ref.1), custom_call_target="tpu_custom_call" | custom-call | tf_op jit(solution)/shard_map/gather_members/pallas_call | solution.py:109
  146.6 21.9 %band.1 = (f32[1024,1024]{1,0:T(8,128)}, bf16[4,256,1280]{2,1,0:T(8,128)(2,1)}, bf16[4,256,1280]{2,1,0:T(8,128)(2,1)}, f32[8,128]{1,0:T(8,128)}) custom-call(f32[3,512,1024]{2,1,0:T(8,128)} %bitcast.1), custom_call_target="tpu_custom_call" | custom-call | tf_op jit(solution)/shard_map/band/pallas_call | solution.py:177
  168.5 137.1 %products.1 = f32[128,128]{1,0:T(8,128)} custom-call(f32[128,128]{1,0:T(8,128)} %w_ref.1, bf16[4,256,1280]{2,1,0:T(8,128)(2,1)} %get-tuple-element.7.high_ref, bf16[4,256,1280]{2,1,0:T(8,128)(2,1)} %get-tuple-element.8.low_ref, f32[8,128]{1,0:T(8,128)} %get-tuple-element.9.square_ref), custom_call_target="tpu_custom_call" | custom-call | tf_op jit(solution)/shard_map/products/pallas_call | solution.py:300
  305.5 1.5 copy.5

commit v2 on v1

--- a/solution.py
+++ b/solution.py
@@ -29,6 +29,32 @@
     128.0 / (35.0 * math.pi),
 )
 
+ROUTES = (
+    (0x8e4662f1386c2e0b028f46e28008742a0d00000000000874220d00000000000874260f01, 0x8ec662d100000000008e46e2f100000000008e4662f1186c2c01008f46a2b10004220d02, 0x8f466291386c2a0b028f46e291386c2e09028fc62291387c260b028ec66291186c2e0d03, 0x8f4622b1187c220d02004662f1187c2e0f038fc6e2d108642a0b038e4662d1386c220b00, 0x46e29110000000008ec6c0000004220f000046a2e00874220f010046a2f11864260901, 0x8ec662d12000020f010046a2b12000020b030046229118780001038e80000008742e0b03),
+    (0x8fc6a2c00874220d010000000008642e0f0200000000086c260f030000000008642e0b02, 0x8fc6229120000000008ec6a2b120000000008f4622b100000000008e4662913004280100, 0x8fc6a2f1187c220f018fc6001118642a0f018e46e2f108642a0d008fc600110004240101, 0x8e46a2f1386c2e0f0000462291386c220b008ec622f1287c2209018f46229128642a0901, 0x4622b120000000000046000000042a0d010000000000042a09030046400000042e0a00, 0x8fc6a2913000020d00004622d130000001010046a2b13860000000000000000878020f01),
+    (0x86c6e0a008642a110087000000081c3e4f2100000000084c2a150f00426e97186c1a0903, 0x8e46a2b15006af4ba38dfea33130000001e188453ef16f6002040089c62231d97c362b05, 0x8e46e2b108542e09008746a6d3285c120b03874662d12f642fc9018e46e6912004680100, 0x46631028ec3fcf0388c6e0d1786427cf21884666b118e43215028ec6e2f118f4360d02, 0x88fee2710ce6672fe088c67ee008e46e0510c6800011f81c660d11004630d8285c220f0d, 0x8f4522b11d76ac01039ec2a2f000066e1710004ea0d108e0024a00004e30d828041a110d),
+    (0xdec6000008542609038c000000086c364d200045c0000854164b0c00002eb7287c320d00, 0x89c6e2f1e000034fa18fc6227140000000008fc6e27120000001108fc6e2d1684c661510, 0x874622312004260d0386464011e8e41fc9008f46a6d3286c222f238cc6a6b3184c640102, 0x46e0d1281427cd019fc2e6910cf43e09200046a29138f42611000046a6b1087c2e1503, 0x877e20d02cfe6b2d93000000000cf43e031200000018084c1601050046c01808e42a1113, 0x86c5e0b108400001020042e0f1f0000210000000237128f0020104006280180960000113),
+    (0x42e10008441e17e78d43e3731824261123848026f6285c72033000002e77085e2611f1, 0x88f62271f0069b51158bc523111e772e33f18ec5a371cf5eee19ec894d2211f80c621b04, 0x8c802211e85c17c4008e4da4f0e8dfe60d128ecaa6b0ef5f93cb038f0024d1d00463ee00, 0x24d10c6c2a08009efea4f618efebcde7aec226f3386c2fce00888022b1689c7be800, 0x8642a2318fe66f0bf081cd801fff1c6a1302b60030535884622b16b8dec01858d4362b06, 0x42a2f1fd066e1fa39f4663311c700329e70045a150f85f925600d7e372b859e0022323),
+    (0x422210387c1213e6004d8012087c1609e5854aecd608447a472100002cd6284c3e4140, 0x89452230ee600000008f46623170067bc000897ea211e0000202008de222f1c89802071d, 0x860024b01fe7efc2008ece66b21f77922b228c4da651c874522be187002631fffc1a2c00, 0x122876661000884364b148e437c901888024b3ffe43fee00880026933874240000, 0x814260901bf66001f28c8000134f7416270d0000001908446e2712b75e31590fe43e2916, 0x426090ecfe63519396ce6170c900021314004da0f0c8fe5e5108004d715358cc6e8b24),
+    (0x8445217e785c0a05939b4d21d3085c225f01af576033187c36090100002e378ae4121550, 0x8dc7a3595ee763620089c463d15e06ee31f68dc7e1df1f200207e788cda2519818023d1f, 0x8d0026b0084f8b0a008cc9e6512fcc27cc0085cd62b208ec5fce008c002551300423e600, 0xa78026b068fc37d200a646a2d128bfa3f502af5762b3780c37d1e7000024d3180c4c0000, 0x8541e2519006371000b0c273327fcc322f1bb5c731962fe436371cb65ab1b848fc4e2d0a, 0x884aa171e89e3763a186c26110290e3f37c395002311dc4f96070d006231bf195c3e9600),
+    (0xa7c26120084fa20e000043643238541a1f03a68024765a04320b3400002c9618043a0352, 0x8f7562117e1eec010e88c42291df26e2220088e2e2918ee7bf69eb8849a3b119fede2913, 0x8d8020303e67862c009ecd64d108f797ea0086cca4f30ee41a08008d8020f2fef7de2000, 0xa6002551480477e6000042a6d238ffabe600a7002572c8eff3ebf79980241148946bcc00, 0xfec43afdffde2f218382003f525f841a09e10047b03608a42e211ec4da4019d8c43a07f4, 0x9144231159ee2f33ad9ccd61b06e76d801a09fc7a251ed76af6feb99e6707908dc3a911c),
+    (0x2f39382c1615fb004fe5f2783c760b22a7002bb22864060502b5002e5408445a0105, 0x8845e251cecebc00008c7f22d19ee797f51589fe62d13f3ebe1fe88b4c63f149f4da2119, 0x84002631fe7467e6008dcea491f854200000a64a64133ef4620e0086002772c004162e00, 0xa08025b15cffabd600a04ea491687433f7faa60025125817a7e800ae002771781433d000, 0xf1c120517f1617efe9938022571cc4762be7b24470767c547e130fb159f3d728f4060000, 0x85cb62317dce2321b393c7a090edb45f1db19b4ca330b8179e1db198e273d3dd4c5a2719),
+    (0xe98023d05e1c361bf300416c56084c7204000053a5b348341a1305ae0000179834061706, 0x834563d8ee86b801bc8cffa211f007ee3df38d7e2251ffbe2fedf68ecaa331eef44a1716, 0x87cee471c8dc63c8008c4ee251cf4c17e0008dc526121e6c5a0000868024f33e742bcc00, 0xae00001178e7ebd000a14ee0f0081c2bea00ae0020f2688fea1600a5002553d8043fc800, 0xf240bb5e6f0f9b17959b49b31e5fa47e07e5b4cd6416c8bc761b18c0dc001788944a17e6, 0x8a496111cd7e163bbc9acea3d1c946d3a31d96436110d8047703f5c9cfb298488c061328),
+    (0x838020191a4ff61e00004ca3f70b54131c00a1556d57d814de1723a5002c550a14165d49, 0x8a507e5dfe77576600887c7ef0eecfb79000007ee3917fc75bf8008a4de310ee76222fe8, 0x84800010ee7c13ea008d4e2431d84c562c008ccbe692ceb457ea008d0022730f541fe200, 0xac8027d3581ff7f200a20024d02807e7d000a880249288747bbbf4af8024f3f8ffeaae00, 0xf8c061507c465313eb8a5032395cd42e1be6b3c06fd68fd4321de6a1d900179834420400, 0x84c0a1518dde9b67b9984460d1bdfeb75f1992c9e0916f24dff9dcc1e63219d8b4d23514),
+    (0xe8d720751a9c7753e80049a3942aec1e1200aad32db4ca0c1e073dae8000152a0c0a05ce, 0x8af7a3f0cea6db52008a44a3906e7eb772000046a35148b7535c008be2a37189072e2511, 0x86802690c8cfbff20086c923f338446bd2008d482491f84c13e800878026503ee003c800, 0xa8002692a89467c800ae00211068f7e3c400a00026d0081c47d200a1802710181fefd600, 0x897e63ffbbc6273d6785d961d47fbc2629f2bbd331f708943e29f1b5588019f8840a1f1e, 0x99cd63d0cd8eef538591cde311899e3743b399c820b038ef7747c0dfe4b179f82fce3b15),
+    (0xa4d660f75c3c3a3b85000023b40844320600004defd70a440a5339af802d57783c5e470a, 0x8bc421dd5e5e8774008978637ffed6afa600000023115ff7377600006371b12004de3f4b, 0x8500261228c797c60087802bd23e7c1bc400844c2671df7417e200858025f1ee5003e000, 0xe1800012d86463d400a3d125701f3ff3d400898024f1689fbb9e009e80273028ec3bf400, 0x837a61bf3c3d0701f9b55eec548f3c1e2df9bc57a4364ffc522d1da1584011bfbc5e21e4, 0x9acc6131bdb6b801b49d422351a006af3fb097cfa051c8dfd79fdedf6db2f939149a190e),
+    (0x2f1e880f700000ab802d94782c5e4400005700164824020000ab002ff46824021800, 0x8b5421914ebf537a008b0023516f96a3600000002331bf36b400000064801209ee2a1f18, 0xaa0026720f7fb3da00850026720ed003dc0083456590ce7467cc0084802590eec003e400, 0xa18025300fe7efc600ab8020b4880fffda009f8021303f67e7de009f8025d038e7e7d200, 0x82fa23927bd67f078eb2512c170f446221fccb53aed6b8ac0225eaa080001990040227ea, 0x91c8e1b08d2ed801b595c1a150d006ff39a39acc213178375b5ba2d000325ce004c63318),
+    (0xa5002e3288247c01f500002c34c8ac3a1800000000152a9c3e1e00a2002db67add1a1f59, 0x3dd1ae3e4f59ae000023f18efe940000000023f19f872f7e0000000012b9de360200, 0x858028400f2c6be40096802473fed803ee008541e5d1ee141fec0084002513deec57de00, 0xa4802570389c6ff400ad002540089ffbee00910027d17897e3f5cfa88024915f57e3f600, 0xfcff61dc5007670f8583db61f168fc52011eb0dbef976f940e0be5b90033f680047e25eb, 0x954d2390f0068759ae9dc761f0f006a33ba796cd217018c6de39cd006df3f990040a312d),
+    (0xc38021985a8c00000000002c7480040e7a0000000015882c121a00a6002f94982c7e3800, 0x1dde477b7200000023b1aedf180000000023bfbeb77f7800000000117ec6874200, 0xab8027a00e4803ec009d002052eef803ec00820022531ef803c600838025d3eef803c400, 0xa7002740080ffffa00a48027200817f7e800918025301ff7ee3400a28024400f40023400, 0xfa70f5200005400168b94b2f576f2c3a19febf480012bfa44e170bb30000000004763b18, 0x96cca19090000001b89a472050a0061401dc9bc922d1a0073b83b4de8031f96934aa3757),
+    (0x1f50040c0000000031d5000458000000002ff590043a2200a2802dd5b8540e7800, 0x3dff6e171b700000000010fe8f6c0000000000106e7f237a0000000010c9c7bf1a00, 0x9d8028000f6003e000848029000eb803e400000020600ea800000082002492ded003fc00, 0xa98026e0088c73e800af8000000000039200908000000000038200a08025200f3803ae00, 0xf5f7000000000001a8b6d733d3dfd40239fbb357001240000223fdb280000000000001fa, 0x4c000000000000009c4cc00000069799a59940a3f0800757bbdddd8030391004f61d20),
+    (0x15400448000000002df4400000000000000017f000000000a08000153004540000, 0xe37477600000000000eb7380000000000000efe9400000000001cbed6480000, 0x25800e5003e200000020200e90000000000000000eb8000000000024a00eb003c000, 0xaf802640000003f000ac800000000003d800000000000000000000a98000000000023600, 0xf38000000000031800bb57a8936fac7801f8b854400000000001fe000000000000000112, 0x94c8c0000006c8000094c000000007d001d60000001980055c012b),
+    (0x2fd6e00000000000000014b000000000000000179000000000a78000187004e40000, 0x11de2e8b5c00000000000e2f580000000000000ebf1400000000000000075c0000, 0x2b400ff800000000002a600000000000000000000000000000000025200e2003c600, 0xa5802580000003e200ae8000000000000000a78000000000000000a78000000000038600, 0x1750051ead730000001e20050000000000000000000000000000001e9, 0x920000000006980000934b000000073001ccdc5bc0000000000000),
+    (0x150000000000000000156000000000000000148000000000000000159000000000, 0x116ed7280000000000000e97040000000000000007480000000000000006c00000, 0xed0000000000000000000000000000000000000000000000025600e6003c200, 0xa20025e00000000000ac0000000000000000000000000000000000aa8000000000039a00, 0x55eb924000000000004cc00000000000000000000000000001fb, 0x7c00000944880000007c401cf000000000000000000),
+    (0x157000000000000000000000000000000000000000000000000000000000000000, 0xeaf740000000000000ea0000000000000000007180000000000000000000000, 0xe28000000, 0xa38000000000000000000000000000000000000000000000000000a68000000000000000, 0x56800000000000000053c0000000000000000000000000000000, 0x904b800000077001ef000000000000000000),
+    (0x156000000000000000000000000000000000000000000000000000000000000000, 0x0, 0xe08000000, 0xa90000000000000000000000000000000000000000000000000000000000000000000000, 0x57c0000000000000000000000000000000000000000000000000, 0x980000000000000000000000000000000000),
+    (0x153000000000000000000000000000000000000000000000000000000000000000, 0x0, 0xe78000000, 0xa40000000000000000000000000000000000000000000000000000000000000000000000, 0x0, 0x0),
+)
+
 
 def here():
     return lax.axis_index("row"), lax.axis_index("col")
@@ -62,60 +88,151 @@
     )
 
 
-def gather_kernel(x_ref, out_ref, send_row, send_need, recv):
+DIRECTIONS = ((1, 0, 0), (-1, 0, 0), (0, 1, 0), (0, -1, 0), (0, 0, 1), (0, 0, -1))
+QUARTER = MEMBERS // ROWS // 4
+LAG = 2
+
+
+def place_of(i):
+    return (i % 8) // 4, i % 4, i // 8
+
+
+def arrivals():
+    table = []
+    for sends in ROUTES:
+        by_direction = []
+        for (dx, dy, dz), packed in zip(DIRECTIONS, sends):
+            entries = []
+            for i in range(32):
+                x, y, z = place_of(i)
+                fx, fy, fz = (x - dx) % 4, (y - dy) % 4, (z - dz) % 4
+                entry = packed >> (9 * (fz * 8 + (fx % 2) * 4 + fy)) & 511
+                if entry:
+                    pair = (fx // 2) * 4 + fz + (entry >> 5 & 7)
+                    entry = 256 | (pair - z) % 8 << 5 | entry & 31
+                entries.append(entry)
+            by_direction.append(entries)
+        table.append(by_direction)
+    return table
+
+
+def departures():
+    return [[[packed >> (9 * i) & 511 for i in range(32)] for packed in sends] for sends in ROUTES]
+
+
+def words(table):
+    return [
+        [[d[i] | e[i] << 9 | f[i] << 18 for i in range(32)] for d, e, f in (sends[:3], sends[3:])]
+        for sends in table
+    ]
+
+
+def looked_up(values, bits):
+    if len(set(values)) == 1:
+        return jnp.int32(values[0])
+    low = looked_up(values[: len(values) // 2], bits[:-1])
+    high = looked_up(values[len(values) // 2 :], bits[:-1])
+    return jnp.where(bits[-1], high, low)
+
+
+def gather_kernel(x_ref, out_ref, send, recv, across_send, across_recv, own_sem):
     r, c = here()
+    core = lax.rem(c, 2)
+    pair = lax.div(c, 2)
+    z = lax.rem(pair, 4)
+    x = lax.div(pair, 4) * 2 + lax.div(r, 4)
+    y = lax.rem(r, 4)
+    first = core == 0
+    sign = 1 - 2 * core
+    index = jnp.where(first, z * 8 + r, (3 - z) * 8 + 7 - r)
+    bits = [lax.rem(lax.div(index, 2**b), 2) == 1 for b in range(5)]
+
+    def neighbour(direction):
+        dx, dy, dz = DIRECTIONS[direction]
+        nx, ny, nz = (lax.rem(v + sign * d + 4, 4) for v, d in ((x, dx), (y, dy), (z, dz)))
+        return lax.rem(nx, 2) * 4 + ny, lax.div(nx, 2) * 8 + nz * 2 + core
+
+    sides = [neighbour(d) for d in range(6)]
+    other = (r, c + sign)
+
+    across = lax.rem(2 * pair - 4 + r + 2 - core - lax.rem(r, 2) + COLS, COLS)
+
+    own = pltpu.make_async_copy(x_ref, out_ref.at[c, r], own_sem)
+    own.start()
     barrier = pltpu.get_barrier_semaphore()
-    for shift in range(1, ROWS):
-        pl.semaphore_signal(barrier, inc=1, device_id=at(lax.rem(r + shift, ROWS), c), device_id_type=MESH)
-    for panel in range(2):
-        block = lax.rem(c + r - 4 + panel + COLS, COLS)
-        for row in range(ROWS):
-            own = None
-            if row == 4 - panel:
-                own = r == row
-
-            def greet(row=row, block=block):
-                pl.semaphore_signal(barrier, inc=1, device_id=at(row, block), device_id_type=MESH)
-
-            unless(own, greet)
-    pl.semaphore_wait(barrier, 7 + 16 - jnp.where((r == 3) | (r == 4), 1, 0))
-
-    for row, col, panel, own in reached(r, c):
-        def go(row=row, col=col, panel=panel):
-            copied(x_ref, out_ref.at[1 + panel, r], send_need.at[panel, row], recv.at[1 + panel, r], row, col).start()
-
-        unless(own, go)
-        if own is not None:
-            @pl.when(own)
-            def _(panel=panel):
-                pltpu.make_async_copy(x_ref, out_ref.at[1 + panel, r], recv.at[1 + panel, r]).start()
-    for shift in range(1, ROWS):
-        copied(x_ref, out_ref.at[0, r], send_row.at[shift], recv.at[0, r], lax.rem(r + shift, ROWS), c).start()
-    pltpu.make_async_copy(x_ref, out_ref.at[0, r], recv.at[0, r]).start()
-
-    for row, col, panel, own in reached(r, c):
-        def done(row=row, col=col, panel=panel):
-            copied(x_ref, out_ref.at[1 + panel, r], send_need.at[panel, row], recv.at[1 + panel, r], row, col).wait_send()
-
-        unless(own, done)
-    for shift in range(1, ROWS):
-        copied(x_ref, out_ref.at[0, r], send_row.at[shift], recv.at[0, r], lax.rem(r + shift, ROWS), c).wait_send()
-    for panel in range(3):
-        for row in range(ROWS):
-            pltpu.make_async_copy(x_ref, out_ref.at[panel, row], recv.at[panel, row]).wait()
+    for row, col in sides + [other]:
+        pl.semaphore_signal(barrier, inc=1, device_id=at(row, col), device_id_type=MESH)
+    pl.semaphore_wait(barrier, 7)
+    own.wait()
+
+    def unit(entry):
+        relative = lax.rem(lax.div(entry, 32), 8)
+        row = lax.rem(lax.div(entry, 4), 8)
+        block = lax.rem(pair + sign * relative + 8, 8) * 2 + core
+        row = jnp.where(first, row, 7 - row)
+        quarter = pl.multiple_of(lax.rem(entry, 4) * QUARTER, QUARTER)
+        return block, out_ref.at[block, row, pl.ds(quarter, QUARTER)]
+
+    def entries(table):
+        found = []
+        for word in table:
+            word = looked_up(word, bits)
+            found += [lax.rem(word, 512), lax.rem(lax.div(word, 512), 512), lax.div(word, 512 * 512)]
+        return found
+
+    whole = out_ref.at[c, r]
+    piece = out_ref.at[c, r, pl.ds(0, QUARTER)]
+
+    def pass_across(block, ref):
+        @pl.when(block == across)
+        def _():
+            copied(ref, ref, across_send, across_recv, *other).start()
+
+    def take(step):
+        for d, entry in enumerate(entries(incoming[step])):
+            @pl.when(entry >= 256)
+            def _(d=d, entry=entry):
+                block, ref = unit(entry)
+                pltpu.make_async_copy(ref, ref, recv.at[step, d]).wait()
+                pass_across(block, ref)
+
+    incoming, outgoing = words(arrivals()), words(departures())
+    pass_across(c, whole)
+    rounds = len(ROUTES)
+    for step in range(rounds + LAG):
+        if step >= LAG:
+            take(step - LAG)
+        if step < rounds:
+            for d, entry in enumerate(entries(outgoing[step])):
+                @pl.when(entry >= 256)
+                def _(d=d, entry=entry):
+                    _, ref = unit(entry)
+                    copied(ref, ref, send.at[step, d], recv.at[step, d], *sides[d]).start()
+    for step in range(rounds):
+        for d, entry in enumerate(entries(outgoing[step])):
+            @pl.when(entry >= 256)
+            def _(d=d):
+                copied(piece, piece, send.at[step, d], recv.at[step, d], *sides[d]).wait_send()
+    block = out_ref.at[c]
+    sent = copied(block, block, across_send, across_recv, *other)
+    sent.wait_send()
+    sent.wait_recv()
 
 
 def gathered(block):
+    rounds = len(ROUTES)
     return pl.pallas_call(
         gather_kernel,
         name="gather_members",
-        out_shape=jax.ShapeDtypeStruct((3, ROWS, MEMBERS // ROWS, BLOCK), jnp.float32),
+        out_shape=jax.ShapeDtypeStruct((COLS, ROWS, MEMBERS // ROWS, BLOCK), jnp.float32),
         in_specs=[pl.BlockSpec(memory_space=pl.ANY)],
         out_specs=pl.BlockSpec(memory_space=pl.ANY),
         scratch_shapes=[
-            pltpu.SemaphoreType.DMA((ROWS,)),
-            pltpu.SemaphoreType.DMA((2, ROWS)),
-            pltpu.SemaphoreType.DMA((3, ROWS)),
+            pltpu.SemaphoreType.DMA((rounds, 6)),
+            pltpu.SemaphoreType.DMA((rounds, 6)),
+            pltpu.SemaphoreType.DMA,
+            pltpu.SemaphoreType.DMA,
+            pltpu.SemaphoreType.DMA,
         ],
         compiler_params=pltpu.CompilerParams(collective_id=1, has_side_effects=True),
     )(block)
@@ -140,9 +257,14 @@
     return rows[:, :BLOCK]
 
 
-def band_kernel(x_ref, local_ref, high_ref, low_ref, square_ref, xh, xl):
-    r, _ = here()
+def band_kernel(all_ref, local_ref, high_ref, low_ref, square_ref, x_ref, xh, xl, sems):
+    r, c = here()
+    loads = []
+    for panel, block in enumerate((c, lax.rem(c + r - 4 + COLS, COLS), lax.rem(c + r - 3 + COLS, COLS))):
+        loads.append(pltpu.make_async_copy(all_ref.at[block], x_ref.at[panel], sems.at[panel]))
+        loads[-1].start()
     for panel in range(3):
+        loads[panel].wait()
         for first in range(0, BLOCK, SUB):
             values = x_ref[panel, :, first : first + SUB]
             centered = values - jnp.sum(values, 0, keepdims=True) / MEMBERS
@@ -183,11 +305,13 @@
             jax.ShapeDtypeStruct((BLOCK // SUB, SUB, SPAN), jnp.bfloat16),
             jax.ShapeDtypeStruct((8, 128), jnp.float32),
         ),
-        in_specs=[pl.BlockSpec(memory_space=pltpu.VMEM)],
+        in_specs=[pl.BlockSpec(memory_space=pl.ANY)],
         out_specs=[pl.BlockSpec(memory_space=pltpu.VMEM)] * 4,
         scratch_shapes=[
+            pltpu.VMEM((3, MEMBERS, BLOCK), jnp.float32),
             pltpu.VMEM((MEMBERS, 3 * BLOCK), jnp.bfloat16),
             pltpu.VMEM((MEMBERS, 3 * BLOCK), jnp.bfloat16),
+            pltpu.SemaphoreType.DMA((3,)),
         ],
         compiler_params=pltpu.CompilerParams(vmem_limit_bytes=VMEM_LIMIT),
     )(panels)
@@ -328,7 +452,7 @@
 
 
 def on_device(perturbations, probes):
-    panels = gathered(perturbations).reshape(3, MEMBERS, BLOCK)
+    panels = gathered(perturbations).reshape(COLS, MEMBERS, BLOCK)
     localized, high, low, squares = banded(panels)
     return localized, sampler(probes, high, low, squares)
 

time: 313 us -> 207 us (0.66); the launches traced: 307 us -> 207 us
  Pallas kernels: 305 us -> 204 us
    pallas_call x1, Pallas kernels: 146 us -> 62.8 us  [gathered(): pl.pallas_call(gather_kernel, name='gather_members', out_shape=jax.ShapeD...]
    pallas_call x1, Pallas kernels: 137 us -> 119 us  [sampler(): pl.pallas_call(product_kernel, name='products', out_shape=jax.ShapeDtypeS...]
where the time goes in v2:
time: 207 us
  Pallas kernels  204 us (99%)
    pallas_call x1, Pallas kernels, sampler(): pl.pallas_call(product_kernel, name='products', out_shape=jax.ShapeDtypeS...  119 us
    pallas_call x1, Pallas kernels, gathered(): pl.pallas_call(gather_kernel, name='gather_members', out_shape=jax.ShapeD...  62.8 us
    pallas_call x1, Pallas kernels, banded(): pl.pallas_call(band_kernel, name='band', out_shape=(jax.ShapeDtypeStruct(...  23.1 us

profile of v2, /device:TPU:26, one launch (start us, length us, event | category | flops | bytes accessed | tf_op | source)
XLA Modules:
  0.0 206.5 jit_solution(3367172190674086735)
XLA Ops:
  0.6 62.8 %gather_members.1 = f32[16,8,64,1024]{3,2,1,0:T(8,128)} custom-call(f32[64,1024]{1,0:T(8,128)} %x_ref.1), custom_call_target="tpu_custom_call" | custom-call | tf_op jit(solution)/shard_map/gather_members/pallas_call | solution.py:224
  63.4 23.1 %band.1 = (f32[1024,1024]{1,0:T(8,128)}, bf16[4,256,1280]{2,1,0:T(8,128)(2,1)}, bf16[4,256,1280]{2,1,0:T(8,128)(2,1)}, f32[8,128]{1,0:T(8,128)}) custom-call(f32[16,512,1024]{2,1,0:T(8,128)} %bitcast.1), custom_call_target="tpu_custom_call" | custom-call | tf_op jit(solution)/shard_map/band/pallas_call | solution.py:299
  86.5 118.5 %products.1 = f32[128,128]{1,0:T(8,128)} custom-call(f32[128,128]{1,0:T(8,128)} %w_ref.1, bf16[4,256,1280]{2,1,0:T(8,128)(2,1)} %get-tuple-element.7.high_ref, bf16[4,256,1280]{2,1,0:T(8,128)(2,1)} %get-tuple-element.8.low_ref, f32[8,128]{1,0:T(8,128)} %get-tuple-element.9.square_ref), custom_call_target="tpu_custom_call" | custom-call | tf_op jit(solution)/shard_map/products/pallas_call | solution.py:424
  205.0 1.5 copy.5

commit v3 on v2

--- a/solution.py
+++ b/solution.py
@@ -64,16 +64,6 @@
     return {"row": row, "col": col}
 
 
-def reached(r, c):
-    found = []
-    for panel in range(2):
-        for row in range(ROWS):
-            col = lax.rem(c + (4 - panel) - row + 2 * COLS, COLS)
-            own = (r == row) if row == 4 - panel else None
-            found.append((row, col, panel, own))
-    return found
-
-
 def unless(own, step):
     if own is None:
         step()
@@ -257,12 +247,94 @@
     return rows[:, :BLOCK]
 
 
-def band_kernel(all_ref, local_ref, high_ref, low_ref, square_ref, x_ref, xh, xl, sems):
+def main_kernel(
+    all_ref, w_ref, local_out, out_ref,
+    x_ref, xh, xl, band_ref, high_ref, low_ref, local_ref,
+    iterate, window, wide, parts, sums, square_ref, row_squares, col_squares, row_total,
+    load_sem, store_sem, send_w, recv_w, send_x, send_y, recv_y, send_r, recv_r, send_c, recv_c,
+):
     r, c = here()
+    core = lax.rem(c, 2)
+    pair = lax.div(c, 2)
     loads = []
     for panel, block in enumerate((c, lax.rem(c + r - 4 + COLS, COLS), lax.rem(c + r - 3 + COLS, COLS))):
-        loads.append(pltpu.make_async_copy(all_ref.at[block], x_ref.at[panel], sems.at[panel]))
+        loads.append(pltpu.make_async_copy(all_ref.at[block], x_ref.at[panel], load_sem.at[panel]))
         loads[-1].start()
+
+    other = (r, c + 1 - 2 * core)
+    shared = 1 - core
+    passes = core == lax.rem(r + 1, 2)
+
+    def targets():
+        found = []
+        for s in range(4):
+            row = 2 * s + core
+            found.append((3 * s, row, lax.rem(pair + 2 - s + 8, 8) * 2, 0, (core == 0) & (r == 4) if s == 2 else None))
+            found.append((3 * s + 1, row, lax.rem(pair + 1 - s + 8, 8) * 2 + 1, 1, (core == 1) & (r == 3) if s == 1 else None))
+            row = 2 * s + 1 - core
+            own = None
+            if s in (1, 2):
+                own = (core == s - 1) & (r == row)
+            found.append((3 * s + 2, row, lax.rem(pair + 1 - s + core + 8, 8) * 2 + core, shared, own))
+        return found
+
+    barrier = pltpu.get_barrier_semaphore()
+
+    def greet(row, col):
+        pl.semaphore_signal(barrier, inc=1, device_id=at(row, col), device_id_type=MESH)
+
+    for shift in range(1, ROWS):
+        greet(lax.rem(r + shift, ROWS), c)
+    for shift in range(1, COLS):
+        greet(r, lax.rem(c + shift, COLS))
+    greet(*other)
+    outer = lax.rem(c + r - 4 + core + COLS, COLS)
+    inner = lax.rem(c + r - 3 - core + COLS, COLS)
+    for row in range(ROWS):
+        unless((outer == c) & (r == row), lambda row=row: greet(row, outer))
+        unless(jnp.logical_not(passes) | ((inner == c) & (r == row)), lambda row=row: greet(row, inner))
+    pl.semaphore_wait(barrier, 7 + 15 + 1 + 12 - jnp.where((r == 3) | (r == 4), 1, 0))
+
+    def send_iterate(step, source):
+        for slot, row, col, panel, own in targets():
+            def go(slot=slot, row=row, col=col, panel=panel):
+                copied(source, window.at[step, panel, r], send_w.at[step, slot], recv_w.at[step, panel, r], row, col).start()
+
+            unless(own, go)
+            if own is not None:
+                @pl.when(own)
+                def _(panel=panel):
+                    pltpu.make_async_copy(source, window.at[step, panel, r], recv_w.at[step, panel, r]).start()
+
+    def take_iterate(step):
+        @pl.when(passes)
+        def _():
+            for row in range(ROWS):
+                block = window.at[step, shared, row]
+                pltpu.make_async_copy(block, block, recv_w.at[step, shared, row]).wait()
+                there = window.at[step, 1 - shared, row]
+                copied(block, there, send_x.at[step, row], recv_w.at[step, 1 - shared, row], *other).start()
+                split(step, shared, row)
+        for row in range(ROWS):
+            landed(step, core, row)
+        @pl.when(jnp.logical_not(passes))
+        def _():
+            for row in range(ROWS):
+                landed(step, shared, row)
+
+    def split(step, panel, row):
+        high, low = parted(window[step, panel, row])
+        first = pl.multiple_of((panel * ROWS + row) * PIECE, PIECE)
+        wide[pl.ds(first, PIECE), :PIECE] = high
+        wide[pl.ds(first, PIECE), PIECE:] = low
+
+    def landed(step, panel, row):
+        block = window.at[step, panel, row]
+        pltpu.make_async_copy(block, block, recv_w.at[step, panel, row]).wait()
+        split(step, panel, row)
+
+    send_iterate(0, w_ref)
+
     for panel in range(3):
         loads[panel].wait()
         for first in range(0, BLOCK, SUB):
@@ -286,91 +358,30 @@
         over = ((0,), (0,))
         gram = dotted(rows_h, cols_h, over) + (dotted(rows_h, cols_l, over) + dotted(rows_l, cols_h, over))
         band = gram * taper
+        band_ref[tile] = band
         high, low = parted(band)
         high_ref[tile] = high
         low_ref[tile] = low
         squares = squares + jnp.sum((band * band).reshape(SUB // 8, 8, SPAN // 128, 128), (0, 2))
-        for group in range(0, SUB, 8):
-            local_ref[first + group : first + group + 8, :] = skewed(band[group : group + 8, :], group)
     square_ref[...] = squares
-
-
-def banded(panels):
-    return pl.pallas_call(
-        band_kernel,
-        name="band",
-        out_shape=(
-            jax.ShapeDtypeStruct((BLOCK, BLOCK), jnp.float32),
-            jax.ShapeDtypeStruct((BLOCK // SUB, SUB, SPAN), jnp.bfloat16),
-            jax.ShapeDtypeStruct((BLOCK // SUB, SUB, SPAN), jnp.bfloat16),
-            jax.ShapeDtypeStruct((8, 128), jnp.float32),
-        ),
-        in_specs=[pl.BlockSpec(memory_space=pl.ANY)],
-        out_specs=[pl.BlockSpec(memory_space=pltpu.VMEM)] * 4,
-        scratch_shapes=[
-            pltpu.VMEM((3, MEMBERS, BLOCK), jnp.float32),
-            pltpu.VMEM((MEMBERS, 3 * BLOCK), jnp.bfloat16),
-            pltpu.VMEM((MEMBERS, 3 * BLOCK), jnp.bfloat16),
-            pltpu.SemaphoreType.DMA((3,)),
-        ],
-        compiler_params=pltpu.CompilerParams(vmem_limit_bytes=VMEM_LIMIT),
-    )(panels)
-
-
-def product_kernel(
-    w_ref, high_ref, low_ref, square_ref, out_ref,
-    iterate, window, wide, parts, sums, row_squares, col_squares, row_total,
-    send_w, recv_w, send_y, recv_y, send_r, recv_r, send_c, recv_c,
-):
-    r, c = here()
-    barrier = pltpu.get_barrier_semaphore()
-    for shift in range(1, ROWS):
-        pl.semaphore_signal(barrier, inc=1, device_id=at(lax.rem(r + shift, ROWS), c), device_id_type=MESH)
-    for shift in range(1, COLS):
-        pl.semaphore_signal(barrier, inc=1, device_id=at(r, lax.rem(c + shift, COLS)), device_id_type=MESH)
-    for panel in range(2):
-        block = lax.rem(c + r - 4 + panel + COLS, COLS)
-        for row in range(ROWS):
-            own = (r == row) if row == 4 - panel else None
-
-            def greet(row=row, block=block):
-                pl.semaphore_signal(barrier, inc=1, device_id=at(row, block), device_id_type=MESH)
-
-            unless(own, greet)
-    pl.semaphore_wait(barrier, 7 + 15 + 16 - jnp.where((r == 3) | (r == 4), 1, 0))
-
-    def send_iterate(step, source):
-        for row, col, panel, own in reached(r, c):
-            def go(row=row, col=col, panel=panel):
-                copied(source, window.at[step, panel, r], send_w.at[step, panel, row], recv_w.at[step, panel, r], row, col).start()
-
-            unless(own, go)
-            if own is not None:
-                @pl.when(own)
-                def _(panel=panel):
-                    pltpu.make_async_copy(source, window.at[step, panel, r], recv_w.at[step, panel, r]).start()
 
     for shift in range(1, ROWS):
         copied(square_ref, row_squares.at[r], send_r.at[shift], recv_r.at[r], lax.rem(r + shift, ROWS), c).start()
     pltpu.make_async_copy(square_ref, row_squares.at[r], recv_r.at[r]).start()
-    send_iterate(0, w_ref)
-    for row in range(ROWS):
-        pltpu.make_async_copy(square_ref, row_squares.at[row], recv_r.at[row]).wait()
-    row_total[...] = jnp.sum(row_squares[...], 0)
-    for shift in range(1, COLS):
-        copied(row_total, col_squares.at[c], send_c.at[shift], recv_c.at[c], r, lax.rem(c + shift, COLS)).start()
-    pltpu.make_async_copy(row_total, col_squares.at[c], recv_c.at[c]).start()
+
+    stores = []
+
+    def skew(tile):
+        first = tile * SUB
+        for group in range(0, SUB, 8):
+            local_ref[first + group : first + group + 8, :] = skewed(band_ref[tile, group : group + 8, :], group)
+        stores.append(pltpu.make_async_copy(local_ref.at[first : first + SUB], local_out.at[first : first + SUB], store_sem.at[tile]))
+        stores[-1].start()
 
     total = None
     summed = power_terms[0] * w_ref[...]
     for step in range(STEPS):
-        for panel in range(2):
-            for row in range(ROWS):
-                pltpu.make_async_copy(w_ref, window.at[step, panel, row], recv_w.at[step, panel, row]).wait()
-                high, low = parted(window[step, panel, row])
-                first = (panel * ROWS + row) * PIECE
-                wide[first : first + PIECE, :PIECE] = high
-                wide[first : first + PIECE, PIECE:] = low
+        take_iterate(step)
         for tile in range(BLOCK // SUB):
             first = tile * SUB
             over = ((1,), (0,))
@@ -386,33 +397,49 @@
 
                 unless(r == row, go)
         if step == 0:
+            for row in range(ROWS):
+                pltpu.make_async_copy(square_ref, row_squares.at[row], recv_r.at[row]).wait()
+            row_total[...] = jnp.sum(row_squares[...], 0)
+            for shift in range(1, COLS):
+                copied(row_total, col_squares.at[c], send_c.at[shift], recv_c.at[c], r, lax.rem(c + shift, COLS)).start()
+            pltpu.make_async_copy(row_total, col_squares.at[c], recv_c.at[c]).start()
+        if step < 2:
+            skew(2 * step)
+        if step == 0:
             for col in range(COLS):
                 pltpu.make_async_copy(row_total, col_squares.at[col], recv_c.at[col]).wait()
             total = jnp.sum(jnp.sum(col_squares[...], 0), keepdims=True) / STATES
         vector = parts[step, pl.ds(pl.multiple_of(r * PIECE, PIECE), PIECE), :]
         for row in range(ROWS):
-            def landed(row=row):
+            def arrived(row=row):
                 pltpu.make_async_copy(w_ref, sums.at[step, row], recv_y.at[step, row]).wait()
 
-            unless(r == row, landed)
+            unless(r == row, arrived)
             vector = vector + jnp.where(r == row, 0.0, sums[step, row])
         vector = vector / total
         summed = summed + power_terms[step + 1] * vector
         if step < STEPS - 1:
             iterate[step] = vector
             send_iterate(step + 1, iterate.at[step])
+            skew(2 * step + 1)
     out_ref[...] = jnp.sqrt(total) * summed
 
+    for copy in stores:
+        copy.wait()
     for shift in range(1, ROWS):
         copied(square_ref, row_squares.at[r], send_r.at[shift], recv_r.at[r], lax.rem(r + shift, ROWS), c).wait_send()
     for shift in range(1, COLS):
         copied(row_total, col_squares.at[c], send_c.at[shift], recv_c.at[c], r, lax.rem(c + shift, COLS)).wait_send()
     for step in range(STEPS):
-        for row, col, panel, own in reached(r, c):
-            def sent(row=row, col=col, panel=panel):
-                copied(w_ref, window.at[step, panel, r], send_w.at[step, panel, row], recv_w.at[step, panel, r], row, col).wait_send()
+        for slot, row, col, panel, own in targets():
+            def sent(slot=slot, row=row, col=col, panel=panel):
+                copied(w_ref, window.at[step, panel, r], send_w.at[step, slot], recv_w.at[step, panel, r], row, col).wait_send()
 
             unless(own, sent)
+        @pl.when(passes)
+        def _(step=step):
+            for row in range(ROWS):
+                copied(w_ref, window.at[step, core, row], send_x.at[step, row], recv_w.at[step, core, row], *other).wait_send()
         for row in range(ROWS):
             def gone(row=row):
                 copied(w_ref, sums.at[step, r], send_y.at[step, row], recv_y.at[step, r], row, c).wait_send()
@@ -420,24 +447,38 @@
             unless(r == row, gone)
 
 
-def sampler(probes, high, low, squares):
+def band_and_sample(members, probes):
     return pl.pallas_call(
-        product_kernel,
-        name="products",
-        out_shape=jax.ShapeDtypeStruct((PIECE, PIECE), jnp.float32),
-        in_specs=[pl.BlockSpec(memory_space=pltpu.VMEM)] * 4,
-        out_specs=pl.BlockSpec(memory_space=pltpu.VMEM),
+        main_kernel,
+        name="band_and_sample",
+        out_shape=(
+            jax.ShapeDtypeStruct((BLOCK, BLOCK), jnp.float32),
+            jax.ShapeDtypeStruct((PIECE, PIECE), jnp.float32),
+        ),
+        in_specs=[pl.BlockSpec(memory_space=pl.ANY), pl.BlockSpec(memory_space=pltpu.VMEM)],
+        out_specs=[pl.BlockSpec(memory_space=pl.ANY), pl.BlockSpec(memory_space=pltpu.VMEM)],
         scratch_shapes=[
+            pltpu.VMEM((3, MEMBERS, BLOCK), jnp.float32),
+            pltpu.VMEM((MEMBERS, 3 * BLOCK), jnp.bfloat16),
+            pltpu.VMEM((MEMBERS, 3 * BLOCK), jnp.bfloat16),
+            pltpu.VMEM((BLOCK // SUB, SUB, SPAN), jnp.float32),
+            pltpu.VMEM((BLOCK // SUB, SUB, SPAN), jnp.bfloat16),
+            pltpu.VMEM((BLOCK // SUB, SUB, SPAN), jnp.bfloat16),
+            pltpu.VMEM((BLOCK, BLOCK), jnp.float32),
             pltpu.VMEM((STEPS - 1, PIECE, PIECE), jnp.float32),
             pltpu.VMEM((STEPS, 2, ROWS, PIECE, PIECE), jnp.float32),
             pltpu.VMEM((2 * BLOCK, 2 * PIECE), jnp.bfloat16),
             pltpu.VMEM((STEPS, BLOCK, PIECE), jnp.float32),
             pltpu.VMEM((STEPS, ROWS, PIECE, PIECE), jnp.float32),
+            pltpu.VMEM((8, 128), jnp.float32),
             pltpu.VMEM((ROWS, 8, 128), jnp.float32),
             pltpu.VMEM((COLS, 8, 128), jnp.float32),
             pltpu.VMEM((8, 128), jnp.float32),
+            pltpu.SemaphoreType.DMA((3,)),
+            pltpu.SemaphoreType.DMA((BLOCK // SUB,)),
+            pltpu.SemaphoreType.DMA((STEPS, 12)),
             pltpu.SemaphoreType.DMA((STEPS, 2, ROWS)),
-            pltpu.SemaphoreType.DMA((STEPS, 2, ROWS)),
+            pltpu.SemaphoreType.DMA((STEPS, ROWS)),
             pltpu.SemaphoreType.DMA((STEPS, ROWS)),
             pltpu.SemaphoreType.DMA((STEPS, ROWS)),
             pltpu.SemaphoreType.DMA((ROWS,)),
@@ -448,13 +489,11 @@
         compiler_params=pltpu.CompilerParams(
             collective_id=2, has_side_effects=True, vmem_limit_bytes=VMEM_LIMIT
         ),
-    )(probes, high, low, squares)
+    )(members, probes)
 
 
 def on_device(perturbations, probes):
-    panels = gathered(perturbations).reshape(COLS, MEMBERS, BLOCK)
-    localized, high, low, squares = banded(panels)
-    return localized, sampler(probes, high, low, squares)
+    return band_and_sample(gathered(perturbations).reshape(COLS, MEMBERS, BLOCK), probes)
 
 
 def solution(mesh):

time: 207 us -> 180 us (0.87)
  Pallas kernels: 204 us -> 174 us
  local copies, waits for them, and re-layouts: 1.47 us -> 5.45 us
    pallas_call x2 -> x1, Pallas kernels: 142 us -> 111 us  [band_and_sample(): pl.pallas_call(main_kernel, name='band_and_sample', out_shape=(jax.ShapeD...]
    unnamed x1 -> x4, local copies, waits for them, and re-layouts: 1.47 us -> 5.45 us
where the time goes in v3:
time: 180 us
  Pallas kernels  174 us (97%)
  local copies, waits for them, and re-layouts  5.45 us (3%)
    pallas_call x1, Pallas kernels, band_and_sample(): pl.pallas_call(main_kernel, name='band_and_sample', out_shape=(jax.ShapeD...  111 us
    pallas_call x1, Pallas kernels, gathered(): pl.pallas_call(gather_kernel, name='gather_members', out_shape=jax.ShapeD...  62.8 us
    unnamed x4, local copies, waits for them, and re-layouts  5.45 us

profile of v3, /device:TPU:26, one launch (start us, length us, event | category | flops | bytes accessed | tf_op | source)
XLA Modules:
  0.0 180.1 jit_solution(10221930525175511141)
XLA Ops:
  0.6 62.8 %gather_members.1 = f32[16,8,64,1024]{3,2,1,0:T(8,128)} custom-call(f32[64,1024]{1,0:T(8,128)} %x_ref.1), custom_call_target="tpu_custom_call" | custom-call | tf_op jit(solution)/shard_map/gather_members/pallas_call | solution.py:214
  63.4 111.3 %band_and_sample.1 = (f32[1024,1024]{1,0:T(8,128)}, f32[128,128]{1,0:T(8,128)}) custom-call(f32[16,512,1024]{2,1,0:T(8,128)} %bitcast.1, f32[128,128]{1,0:T(8,128)} %w_ref.1), custom_call_target="tpu_custom_call" | custom-call | tf_op jit(solution)/shard_map/band_and_sample/pallas_call | solution.py:451
  174.7 0.0 copy-start
  174.7 4.8 %copy.6 = f32[1024,1024]{1,0:T(8,128)} copy(f32[1024,1024]{1,0:T(8,128)} %get-tuple-element.4) | data formatting | bytes 8388608
  179.5 0.0 copy-done
  179.5 0.6 copy.7
Async XLA Ops:
  174.7 4.8 %copy-start = (f32[128,128]{1,0:T(8,128)S(1)}, f32[128,128]{1,0:T(8,128)}, u32[]{:S(2)}) copy-start(f32[128,128]{1,0:T(8,128)} %get-tuple-element.5) | copy-start | bytes 196612

commit v4 on v3

v4 whole, which is shorter than its diff:
```python
import functools
import math

import jax
import jax.numpy as jnp
from jax import lax
from jax.experimental import pallas as pl
from jax.experimental.pallas import tpu as pltpu
from jax.sharding import PartitionSpec as P

MEMBERS = 512
STATES = 16384
WINDOW = 4096
ROWS = 8
COLS = 16
BLOCK = 1024
PIECE = 128
SUB = 256
SPAN = SUB + BLOCK
STEPS = 3
MESH = pl.DeviceIdType.MESH
VMEM_LIMIT = 58 * 2**20

epsilon = 1e-06
power_terms = (
    2.0 / math.pi - 4.0 / (3.0 * math.pi) - 4.0 / (15.0 * math.pi) - 4.0 / (35.0 * math.pi),
    8.0 / (3.0 * math.pi) + 32.0 / (15.0 * math.pi) + 72.0 / (35.0 * math.pi),
    -32.0 / (15.0 * math.pi) - 192.0 / (35.0 * math.pi),
    128.0 / (35.0 * math.pi),
)

ROUTES = (
    (0x22f1386c260b0000000000086c260d0100000000086c260b0100000000086c2a0d01, 0x8e4622f130000000008ec6a2b100000001008f4662b1087c2c01038ec6a2d130042e0d01, 0x8fc622b1386c220b018ec6e2f1086c260d008fc66291386c2e0f018ec622b1186c2a0903, 0x8ec6e2f1386c2209008ec622d11864260b038fc662f1387c260b038ec6a2f118742a0d00, 0x8ec6629100000001038fc6e2b118742e0d010046a2c008742a0b01004622f1086c2e0b01, 0x8e4622f1286c2a0f038f46a2b12004220b018e4622d1386c24010000468000087c220f03),
    (0x8642e0d0200000000087c2e09000000000008642a0f0300000000087c220b02, 0x8fc662d120000000008f46e2f120000000008ec6229110000000008e46e29120042a0b00, 0x8e46e2912864260d028f4622d1287c220b018f46a2f108742a09028f46e2f128742e0d01, 0x8fc622d1087c2e0d028fc6a2f1387c220f018e46e2b1286c2a0f028e4622b1387c260f03, 0x8f46a2b110000000008e46401138642609020046c000087c220d02000000113864260f02, 0x8fc6a2d11874220b01004622d100042800000046e2b128642c0103000000000864260800),
    (0x87c2a0901000000000874220f03000000000874220d00000000000864260903, 0x8ec6e29100000000008e4622d110000000008fc6a2d130000000008fc662f10000000102, 0x8f4662f1187c2a0f038e4662b118742a09028e46e2b1187c260b008e46a2d1087c220b02, 0x8e4662b128642a0b018e4662b1086c2a0d028f4622d108642e0d008fc6e2d10864220901, 0x46e2d120000000008e800011287c220b03000000000004260800000000112874220d00, 0x8e8022913004260c000046e29130042c00000046a2f10004200101000000000000000000),
    (0x4260b1f844360f0300476311d84caa4f0200452320087ca21305005e6e9708543a0f63, 0x89eea27f1006a34fe18ffebed16f77a8000089fe227f0f680203108f4e2231796c10010d, 0x86c6a2d1f8e416030086c6a2132f742fcb038ecea6b1285c662b0d8fde66d1d8646a2d13, 0x8f4260b17807afcde19e426290187433cb2389c6a6b1181c2209e19e4660d128ec2e1502, 0xffc77eb00007af2f938d802218084c6a2b0dc7c7c0117004660f0dbec770d118543a1503, 0x89c563717d7c174fa39e45e0d1d9680000009f47e0b1f8f43c0105004570d818eca62d20),
    (0x47e271684c3e04000047e21328443e0121004e80130854aa4b0e89deaeb7181cae0720, 0xffc5225f3d66a7490489fee291e00000000089472331ff600215e188c6235159646a0312, 0x86452251cf642e2e008c0026f1e86417cd2386ce2211e8f41fcb0e8dcee231e85c6e2900, 0x8846a0d11877a7c9e29fc2e0900f743e13e18e80229158f43fcbe287dea6b158e43e0a00, 0x8842e0d1cf6000000088c5a25160046e030f0000237830046229e2bf62e25700046e2c00, 0x864762700816a2110489c26091797002110f0045e0f0381caa2902004e30b808e46e290d),
    (0x45e250280432020000000000086436152300000013384cae1521bf5eeed72844160307, 0x89456371e0000207a38846633150000204008862e37f3f7000011189e2e2b1d004662f0e, 0x8c002271e8ffa206009f8026d138541bc912864626d1ff6c13cf038d5ee6b33844662f10, 0x42a0915814362fe38f46e69128ec3611009f0026932877ae2de0885ee6f168fc321200, 0x87c6209f1f780000008cc20011c004622f050000223f384c1e1313005ee21168fc66050f, 0x452090280ea615069fc720f03004a4010e87426311e8ec34010f0062c018285c320706),
    (0x4360f0d8741a000000442133785ca2199d0044c0135a6c161707af5f40160874be1500, 0x8f6d7e1f2007276dc088c5623f7e7fe401c388c4e211c8cfba270b8c4f231119f4762310, 0x8445a4d1084c62091c9e4aa091cf7febec008cca2691d854220de08c4daab13004e22200, 0x4364d218ffebd7e680c2277158f7a3cfe5ae0024d01f0fe3d5f0af5f6290186c3be800, 0xfdc523f61f4e270bed86c40011d004360107b6802131d89c562bf0bce10011f8d46a27f3, 0x47a131edec070bc099caa350d91e7730009d4660d1d816521106d6cfc018d96c5a1517),
    (0x4720501f740211960043e1763854a605240044249378140e092fafdaef57ca652a050b, 0x887623f11006ef68008dffe3d180079401168e7f7ef15007961a009dcde371c91c62130f, 0x848024b0c85c5febf18d4de4f20e7f9a0e00ae4aa4b32f646bcc0086c664b2000427ea00, 0x24b038e7efd3e49647e4f1789fe3e8009980231168ec3233018f5ae0b1780473ee00, 0x8944a390cf0e7f27ef8047ff600f0c2a07eeb65ae3d90f143e331fb844401608dc522915, 0x43e230dde6ef6996964de23029149721099c4a6250e896eb3304d64eb039288c3e0515),
    (0x43223f68541e17e5004d400009741a0b2600000012385c3a0502b7de2f751a7c321f2f, 0x8dc5be5fc006b346008900231170079c00008ac6e2f12fff9c0000886123b1f9ee2e211d, 0x8e8024f20f441fc3f39ecda49228e4122c00aecd62523864162ded854a60d23ff45e2a00, 0x4ae4901f77a3ebf188c3e371681fbbec00af8020d14807e7cdf3975e64b0689c7fea00, 0xfcfa21506f165f259fb75abe334f4c7629f3b756ecd6183c32011eb7df401638f4322b1d, 0x8043631188443801ad00436151e90e7c010899c7a150d8840e3716006132f359647e3525),
    (0x45a1b0882c0607e7004a2193b82c864a00000000126845261f2ead5d2ff63a4c36514d, 0x8b77e3115006db55b78a80221d3eefd401f7000023bf6fd787711c9b002331e9c6d22b11, 0x8749a232d8c41bee00844d6673feefd62e008d4de4f1cfd463e60087de24f1cef41bca00, 0xa68026d4089c3ff503a680253438e46bd200a6802750588feff00000002090281c37ca00, 0xf8c1b0760f1e370febb7c07d3fdf9c7a1b0accdbb2791f847a210abde7401718c43607f4, 0x90c1a1b10d5ed801b795412011c0064313b7944e2170c88c4c01b5df62b238e004363111),
    (0x402010981420010b004bc01278343a1a00000000134a143e5129ac002d76ca0cb6174f, 0x88f6a3c00e0f6344008b803fd1ae17d801ff8b7c62518fdfd36000890023d1b914023713, 0x87cee6932e6c13c000964a6633cfd41e22008dcda2d2dfdc1bc400865d2292e8cc53e600, 0xa60026932894261400a78021314f9feff3f4a98026d0380c7beff5a600271148f7a7f400, 0xf77c23118f367305ec885e70596f2c4e0f1800597158b824720715b95c8016c8442a091c, 0x4421908d8ee8018d9bcda05180063f4bb6954de09198564f491cd1e631337994721f04),
    (0x42a3d9683c380000000000138824325400a7800015ca1c361d28ad802d400a148e1800, 0x8ac6a21d5e4ebf74008b002371bee79800008a00231f1ff62c00008b00225c19844e391c, 0x854966f1de4c53e1fc8fc9e8d01ee46be800acc96472184c6fec0094dae4d2df7c17e400, 0xa700256008efe3ee00898026d3180fbff000a60025517f87f7f200a78026d0580803f600, 0xf07dba31df26332382004180170f3c5a15febfc4b1bfff540e0512005e401668cc5e03ff, 0x42e1715006d40181904063311946d7170c994b63d0185c3001b7dee77219d9dcae3b08),
    (0x6d6210e85c161e0000486e7298142a0600a5000015d824320600a4002f94d84c0e1b4b, 0x8d446231de9eb77000000022713e8790000000003e514f9fcf53fa8a803c71698cce191f, 0x8dc9e630ee6467c60087c9a653de5c622800854d20f3e84003ea00845ea652ced4100000, 0xaf0025536ffc33f600a18020f77817b3a9d7a80024b07897a7e800a88024f0781003ce00, 0xfe78793e50065b1b8dbcdd40171fac7233e7bd5f63f9c8e42e2ff6bc5e0000084c0e231e, 0x934aa210e006b001a69b4fa2f00006a319b29ac2a05148479f53b0dc6672b919b6d23336),
    (0x47a03fd83408000000002d54183c0e4600000000122a0c121800a5002fb4f85ca2114c, 0x22bdde96f35e008a00239fde8f6c000000002231dfc6bc01f80000001c0956ce3f07, 0x9dcd2472ef7003ca0087492411d85c67c00087cae632fff80228008c802493dec003c400, 0xa180253e7f8fbbe800a143a1503807ebcc00a100217068ffebd600a98025504c9803d600, 0x82fefb7fc00603019600594017ff34123df9bdd8703f2fac3617fbba60000000043e1ffe, 0x994e22b0f006fc01b194c9e371b006bc01ad80c961f1a8fe4001b3d166b3790954a22723),
    (0x44211608240c000000002db2400416500000000014ca4516112ca7002cd7da1c060000, 0x23b14e2f2f7ba8007ca3f14e57ec00008b803e11af46c3560000000011a95f6b731e, 0x8cc92420087003cc0085802013ee5003e00084802410df4003c800870020f1fed803e200, 0xa78027400f7ff60e00ae0020a008843bc800a00020900887b38a00a00025700f7fb3d400, 0xf6f9801f20062b3d88005d8019df24321ff8bf5d00126f04763be5b5dd000000047239e2, 0x92cde330a0040c01b593c3a2704004b801bb9bc8e291c8d6f401a3d864f398f95c7a692f),
    (0x41e1d76004d4000000000016b0041e4c00000000140a74020000ac802f378a340a1c00, 0x2331beaeff720000003ffdffe7580000000023ff2fcf235800000000114946123c00, 0x8d0026400ff803e80086002452100003c400840020d3ce5003e5fe9d802413fe441fc600, 0xae8026a008f43a1000a80024a008942fd000a18027200f07a3ce00ae0024c00880039200, 0xf87e401e7000032189bbd9c0127fa40a2d1eb9dcc017af740625ecbd5ac00000047e3ff5, 0x9b4c6340000000018e98cc63f070068401a99b47635110000001a6d8ecf1993944f27726),
    (0x406c55f00550000000002c37000408000000000014300406020000002c945a24b21200, 0x235d7eb7236600000023bd2ebf68000000002351b0073c00000000001189fe4e1000, 0x960024400e5003e4008c802292f8c803ee00958024d3de78022e00848022521e50000000, 0xa90027000887fff2009700256008fff2080088800000081473c800a90024800890038800, 0xf3ffc01840067b0376005980000004661910bc59c0178f4c46230cb2d9800000047a1deb, 0x9a4161c000000001a49ac321d1f0000001b892cd221020000001b4d56033f9c004dc0124),
    (0x420015000410000000000017c0048c000000000015000538000000002f15c0052c0000, 0x119e3ef8000000000011fe5f5400000000001170075400000000000009d6c00000, 0x26000e5803ce00000022400000000000000026400f70000000000026200e7003cc00, 0xa0000000000003a800af0000000000038e0081000000000003d200a70025000007bfcc00, 0xfe80000000064311810059000000000001f2b459000000000001fe005e800000000001e8, 0x93ce401190000001a89349000000000001a79a49238000000001a2d5800019f00000013c),
    (0x438015100000000000000015a000000000000000151000000000000000152004000000, 0x11ae377c0000000000000eaf300000000000000007040000000000000007740000, 0xe40000000000000000e70000000000024400000000000000024400ec8000000, 0xa8002720000003b60000000000000003f60000000000000000000090800000000003f200, 0x61f1d7dbe53800000000001fabcd8000000000001e00000000000000001fa, 0x924c8011a0000000009246400000000001a195c9c0000000000000d40033d87000000121),
    (0x17d00000000000000015800000000000000014600000000000000014b000000000, 0xe27680000000000000e077c0000000000000006f400000000001e4000000000, 0xe48000000000000000000000000000000000ef803c800, 0xa08000000000000000000000000000000000000000000000000000a10000000000000000, 0x604018e005ec00000000000000056400000000001f9000000000000000000, 0x1a4000000000000000000df803119e000000122),
    (0x17100000000000000015900000000000000014c000000000, 0xea7700000000000000e4f200000000000000006fc0000000000000000000000, 0x0, 0xa88000000000000000000000000000000000000000000000000000000000000000000000, 0x6200000000000000000000000000000000000000000000000000000000000, 0x1ae000000000000000000dd0000000000000000),
    (0x19d000000000000000000000000000000000147000000000, 0xedf5c0000000000000007240000000000000000000000000000000000000000, 0x0, 0xa10000000000000000000000000000000000000000000000000000000000000000000000, 0x6380000000000000000000000000000000000000000000000000000000000, 0x0),
)


def here():
    return lax.axis_index("row"), lax.axis_index("col")


def at(row, col):
    return {"row": row, "col": col}


def unless(own, step):
    if own is None:
        step()
    else:
        pl.when(jnp.logical_not(own))(step)


def copied(src, dst, send, recv, row, col):
    return pltpu.make_async_remote_copy(
        src_ref=src, dst_ref=dst, send_sem=send, recv_sem=recv,
        device_id=at(row, col), device_id_type=MESH,
    )


DIRECTIONS = ((1, 0, 0), (-1, 0, 0), (0, 1, 0), (0, -1, 0), (0, 0, 1), (0, 0, -1))
QUARTER = MEMBERS // ROWS // 4
LAG = 3


def place_of(i):
    return (i % 8) // 4, i % 4, i // 8


def arrivals():
    table = []
    for sends in ROUTES:
        by_direction = []
        for (dx, dy, dz), packed in zip(DIRECTIONS, sends):
            entries = []
            for i in range(32):
                x, y, z = place_of(i)
                fx, fy, fz = (x - dx) % 4, (y - dy) % 4, (z - dz) % 4
                entry = packed >> (9 * (fz * 8 + (fx % 2) * 4 + fy)) & 511
                if entry:
                    pair = (fx // 2) * 4 + fz + (entry >> 5 & 7)
                    entry = 256 | (pair - z) % 8 << 5 | entry & 31
                entries.append(entry)
            by_direction.append(entries)
        table.append(by_direction)
    return table


def departures():
    return [[[packed >> (9 * i) & 511 for i in range(32)] for packed in sends] for sends in ROUTES]


def words(table):
    return [
        [[d[i] | e[i] << 9 | f[i] << 18 for i in range(32)] for d, e, f in (sends[:3], sends[3:])]
        for sends in table
    ]


def looked_up(values, bits):
    if len(set(values)) == 1:
        return jnp.int32(values[0])
    low = looked_up(values[: len(values) // 2], bits[:-1])
    high = looked_up(values[len(values) // 2 :], bits[:-1])
    return jnp.where(bits[-1], high, low)


def gather_members(x_ref, held, send, recv, across_send, across_recv, own_sem, greet_all):
    r, c = here()
    core = lax.rem(c, 2)
    pair = lax.div(c, 2)
    z = lax.rem(pair, 4)
    x = lax.div(pair, 4) * 2 + lax.div(r, 4)
    y = lax.rem(r, 4)
    first = core == 0
    sign = 1 - 2 * core
    index = jnp.where(first, z * 8 + r, (3 - z) * 8 + 7 - r)
    bits = [lax.rem(lax.div(index, 2**b), 2) == 1 for b in range(5)]

    def neighbour(direction):
        dx, dy, dz = DIRECTIONS[direction]
        nx, ny, nz = (lax.rem(v + sign * d + 4, 4) for v, d in ((x, dx), (y, dy), (z, dz)))
        return lax.rem(nx, 2) * 4 + ny, lax.div(nx, 2) * 8 + nz * 2 + core

    sides = [neighbour(d) for d in range(6)]
    other = (r, c + sign)

    across = lax.div(lax.rem(2 * pair - 4 + r + 2 - core - lax.rem(r, 2) + COLS, COLS), 2)

    own = pltpu.make_async_copy(x_ref, held.at[pair, r], own_sem)
    own.start()
    greet_all(sides)
    own.wait()

    def unit(entry):
        relative = lax.rem(lax.div(entry, 32), 8)
        row = lax.rem(lax.div(entry, 4), 8)
        block = lax.rem(pair + sign * relative + 8, 8)
        row = jnp.where(first, row, 7 - row)
        quarter = pl.multiple_of(lax.rem(entry, 4) * QUARTER, QUARTER)
        return block, row, pl.ds(quarter, QUARTER)

    def entries(table):
        found = []
        for word in table:
            word = looked_up(word, bits)
            found += [lax.rem(word, 512), lax.rem(lax.div(word, 512), 512), lax.div(word, 512 * 512)]
        return found

    piece = held.at[pair, r, pl.ds(0, QUARTER)]

    def pass_across(block, row, part):
        @pl.when(block == across)
        def _():
            copied(held.at[block, row, part], held.at[8, row, part], across_send, across_recv, *other).start()

    def take(step):
        for d, entry in enumerate(entries(incoming[step])):
            @pl.when(entry >= 256)
            def _(d=d, entry=entry):
                block, row, part = unit(entry)
                ref = held.at[block, row, part]
                pltpu.make_async_copy(ref, ref, recv.at[step, d]).wait()
                pass_across(block, row, part)

    incoming, outgoing = words(arrivals()), words(departures())
    pass_across(pair, r, pl.ds(0, MEMBERS // ROWS))
    rounds = len(ROUTES)
    for step in range(rounds + LAG):
        if step >= LAG:
            take(step - LAG)
        if step < rounds:
            for d, entry in enumerate(entries(outgoing[step])):
                @pl.when(entry >= 256)
                def _(d=d, entry=entry):
                    block, row, part = unit(entry)
                    ref = held.at[block, row, part]
                    copied(ref, ref, send.at[step, d], recv.at[step, d], *sides[d]).start()

    def finish():
        for step in range(rounds):
            for d, entry in enumerate(entries(outgoing[step])):
                @pl.when(entry >= 256)
                def _(d=d):
                    copied(piece, piece, send.at[step, d], recv.at[step, d], *sides[d]).wait_send()
        copied(held.at[pair], held.at[8], across_send, across_recv, *other).wait_send()

    copied(held.at[pair], held.at[8], across_send, across_recv, *other).wait_recv()
    return finish


def parted(values):
    high = values.astype(jnp.bfloat16)
    low = (values - high.astype(jnp.float32)).astype(jnp.bfloat16)
    return high, low


def dotted(a, b, dims):
    return lax.dot_general(a, b, (dims, ((), ())), preferred_element_type=jnp.float32)


def skewed(rows, shift):
    sub = lax.broadcasted_iota(jnp.int32, rows.shape, 0)
    if shift:
        rows = pltpu.roll(rows, SPAN - shift, 1)
    for bit in (1, 2, 4):
        rows = jnp.where((sub & bit) != 0, pltpu.roll(rows, SPAN - bit, 1), rows)
    return rows[:, :BLOCK]


def main_kernel(
    members_ref, w_ref, local_out, out_ref,
    held, xh, xl, band_ref, high_ref, low_ref, local_ref,
    iterate, near, window, wide, parts, sums, square_ref, row_squares, col_squares, row_total,
    member_send, member_recv, across_send, across_recv, own_sem, store_sem, send_z, recv_z, send_w, recv_w, send_x, send_y, recv_y, send_r, recv_r, send_c, recv_c,
):
    r, c = here()
    core = lax.rem(c, 2)
    pair = lax.div(c, 2)
    other = (r, c + 1 - 2 * core)
    shared = 1 - core
    passes = core == lax.rem(r + 1, 2)

    def greet_all(sides):
        barrier = pltpu.get_barrier_semaphore()
        partners = list(sides)
        for shift in range(1, ROWS):
            row = lax.rem(r + shift, ROWS)
            partners += [(row, 2 * pair), (row, 2 * pair + 1)]
        for shift in range(1, COLS):
            partners.append((r, lax.rem(c + shift, COLS)))
        for row, col in partners:
            pl.semaphore_signal(barrier, inc=1, device_id=at(row, col), device_id_type=MESH)
        pl.semaphore_wait(barrier, len(partners))

    def to_pairs(step, source, away):
        col = lax.rem(c - 2 * away + COLS, COLS)
        return copied(source, near.at[step, away + 2], send_z.at[step, away + 2], recv_z.at[step, away + 2], r, col)

    def targets(away):
        found = []
        for e in range(3):
            row = 2 * away + core + 2 + e
            valid = None
            if away == -2:
                if e == 0:
                    continue
                valid = core == 1 if e == 1 else None
            if away == 2:
                if e == 2:
                    continue
                valid = core == 0 if e == 1 else None
            there = (1, core, 0)[e]
            panel = (1, shared, 0)[e]
            found.append(((away + 2) * 3 + e, row, there, panel, valid))
        return found

    def share(step, source, away, act):
        for slot, row, there, panel, valid in targets(away):
            own = (row == r) & (there == core)
            go = jnp.logical_not(own)
            if valid is not None:
                own, go = own & valid, go & valid

            @pl.when(go)
            def _(slot=slot, row=row, there=there, panel=panel):
                act(copied(
                    source, window.at[step, panel, r], send_w.at[step, slot], recv_w.at[step, panel, r], row, 2 * pair + there
                ), True)

            @pl.when(own)
            def _(panel=panel):
                act(pltpu.make_async_copy(source, window.at[step, panel, r], recv_w.at[step, panel, r]), False)

    def begin(copy, remote):
        copy.start()

    def send_iterate(step, source):
        for away in (-2, 2, -1, 1):
            to_pairs(step, source, away).start()
        share(step, source, 0, begin)

    def spread_iterate(step):
        for away in (-1, 1, -2, 2):
            block = near.at[step, away + 2]
            pltpu.make_async_copy(block, block, recv_z.at[step, away + 2]).wait()
            share(step, block, away, begin)

    def take_iterate(step):
        @pl.when(passes)
        def _():
            for row in range(ROWS):
                block = window.at[step, shared, row]
                pltpu.make_async_copy(block, block, recv_w.at[step, shared, row]).wait()
                there = window.at[step, 1 - shared, row]
                copied(block, there, send_x.at[step, row], recv_w.at[step, 1 - shared, row], *other).start()
                split(step, shared, row)
        for row in range(ROWS):
            landed(step, core, row)
        @pl.when(jnp.logical_not(passes))
        def _():
            for row in range(ROWS):
                landed(step, shared, row)

    def split(step, panel, row):
        high, low = parted(window[step, panel, row])
        first = pl.multiple_of((panel * ROWS + row) * PIECE, PIECE)
        wide[pl.ds(first, PIECE), :PIECE] = high
        wide[pl.ds(first, PIECE), PIECE:] = low

    def landed(step, panel, row):
        block = window.at[step, panel, row]
        pltpu.make_async_copy(block, block, recv_w.at[step, panel, row]).wait()
        split(step, panel, row)

    finish = gather_members(
        members_ref, held, member_send, member_recv, across_send, across_recv, own_sem, greet_all
    )
    send_iterate(0, w_ref)
    spread_iterate(0)

    near_block = lax.div(lax.rem(c + r - 4 + COLS, COLS), 2)
    far_block = lax.div(lax.rem(c + r - 3 + COLS, COLS), 2)
    odd = lax.rem(r, 2) == 1
    for panel, block in enumerate((pair, jnp.where(odd, 8, near_block), jnp.where(odd, far_block, 8))):
        for first in range(0, BLOCK, SUB):
            values = held[block, :, :, first : first + SUB].reshape(MEMBERS, SUB)
            centered = values - jnp.sum(values, 0, keepdims=True) / MEMBERS
            spread = jnp.sqrt(jnp.sum(centered * centered, 0, keepdims=True) + epsilon)
            high, low = parted(centered / spread)
            lo_at = (panel - 1) * BLOCK + first if panel else 2 * BLOCK + first
            xh[:, lo_at : lo_at + SUB] = high
            xl[:, lo_at : lo_at + SUB] = low
    squares = jnp.zeros((8, 128), jnp.float32)
    gap = lax.broadcasted_iota(jnp.int32, (SUB, SPAN), 1) - lax.broadcasted_iota(jnp.int32, (SUB, SPAN), 0)
    taper = jnp.maximum(0.0, 1.0 - jnp.abs(gap + (r * BLOCK - WINDOW)).astype(jnp.float32) / WINDOW)
    taper = jnp.where((gap >= 0) & (gap < BLOCK), taper, 0.0)
    for tile in range(BLOCK // SUB):
        first = tile * SUB
        rows_h = xh[:, 2 * BLOCK + first : 2 * BLOCK + first + SUB]
        rows_l = xl[:, 2 * BLOCK + first : 2 * BLOCK + first + SUB]
        cols_h = xh[:, first : first + SPAN]
        cols_l = xl[:, first : first + SPAN]
        over = ((0,), (0,))
        gram = dotted(rows_h, cols_h, over) + (dotted(rows_h, cols_l, over) + dotted(rows_l, cols_h, over))
        band = gram * taper
        band_ref[tile] = band
        high, low = parted(band)
        high_ref[tile] = high
        low_ref[tile] = low
        squares = squares + jnp.sum((band * band).reshape(SUB // 8, 8, SPAN // 128, 128), (0, 2))
    square_ref[...] = squares

    for shift in range(1, ROWS):
        copied(square_ref, row_squares.at[r], send_r.at[shift], recv_r.at[r], lax.rem(r + shift, ROWS), c).start()
    pltpu.make_async_copy(square_ref, row_squares.at[r], recv_r.at[r]).start()

    stores = []

    def skew(tile):
        first = tile * SUB
        for group in range(0, SUB, 8):
            local_ref[first + group : first + group + 8, :] = skewed(band_ref[tile, group : group + 8, :], group)
        stores.append(pltpu.make_async_copy(local_ref.at[first : first + SUB], local_out.at[first : first + SUB], store_sem.at[tile]))
        stores[-1].start()

    total = None
    summed = power_terms[0] * w_ref[...]
    for step in range(STEPS):
        take_iterate(step)
        for tile in range(BLOCK // SUB):
            first = tile * SUB
            over = ((1,), (0,))
            both = dotted(high_ref[tile], wide[first : first + SPAN, :], over)
            rest = dotted(low_ref[tile], wide[first : first + SPAN, :PIECE], over)
            parts[step, first : first + SUB, :] = both[:, :PIECE] + (both[:, PIECE:] + rest)
            for row in range(first // PIECE, (first + SUB) // PIECE):
                def go(row=row):
                    copied(
                        parts.at[step, row * PIECE : (row + 1) * PIECE], sums.at[step, r],
                        send_y.at[step, row], recv_y.at[step, r], row, c,
                    ).start()

                unless(r == row, go)
        if step == 0:
            for row in range(ROWS):
                pltpu.make_async_copy(square_ref, row_squares.at[row], recv_r.at[row]).wait()
            row_total[...] = jnp.sum(row_squares[...], 0)
            for shift in range(1, COLS):
                copied(row_total, col_squares.at[c], send_c.at[shift], recv_c.at[c], r, lax.rem(c + shift, COLS)).start()
            pltpu.make_async_copy(row_total, col_squares.at[c], recv_c.at[c]).start()
        if step < 2:
            skew(2 * step)
        if step == 0:
            for col in range(COLS):
                pltpu.make_async_copy(row_total, col_squares.at[col], recv_c.at[col]).wait()
            total = jnp.sum(jnp.sum(col_squares[...], 0), keepdims=True) / STATES
        vector = parts[step, pl.ds(pl.multiple_of(r * PIECE, PIECE), PIECE), :]
        for row in range(ROWS):
            def arrived(row=row):
                pltpu.make_async_copy(w_ref, sums.at[step, row], recv_y.at[step, row]).wait()

            unless(r == row, arrived)
            vector = vector + jnp.where(r == row, 0.0, sums[step, row])
        vector = vector / total
        summed = summed + power_terms[step + 1] * vector
        if step < STEPS - 1:
            iterate[step] = vector
            send_iterate(step + 1, iterate.at[step])
            spread_iterate(step + 1)
            skew(2 * step + 1)
    out_ref[...] = jnp.sqrt(total) * summed

    for copy in stores:
        copy.wait()
    finish()
    for shift in range(1, ROWS):
        copied(square_ref, row_squares.at[r], send_r.at[shift], recv_r.at[r], lax.rem(r + shift, ROWS), c).wait_send()
    for shift in range(1, COLS):
        copied(row_total, col_squares.at[c], send_c.at[shift], recv_c.at[c], r, lax.rem(c + shift, COLS)).wait_send()
    for step in range(STEPS):
        for away in (-2, -1, 1, 2):
            to_pairs(step, w_ref, away).wait_send()
        for away in range(-2, 3):
            share(step, w_ref, away, lambda copy, remote: copy.wait_send() if remote else None)
        @pl.when(passes)
        def _(step=step):
            for row in range(ROWS):
                copied(w_ref, window.at[step, core, row], send_x.at[step, row], recv_w.at[step, core, row], *other).wait_send()
        for row in range(ROWS):
            def gone(row=row):
                copied(w_ref, sums.at[step, r], send_y.at[step, row], recv_y.at[step, r], row, c).wait_send()

            unless(r == row, gone)


def band_and_sample(members, probes):
    return pl.pallas_call(
        main_kernel,
        name="band_and_sample",
        out_shape=(
            jax.ShapeDtypeStruct((BLOCK, BLOCK), jnp.float32),
            jax.ShapeDtypeStruct((PIECE, PIECE), jnp.float32),
        ),
        in_specs=[pl.BlockSpec(memory_space=pl.ANY), pl.BlockSpec(memory_space=pltpu.VMEM)],
        out_specs=[pl.BlockSpec(memory_space=pl.ANY), pl.BlockSpec(memory_space=pltpu.VMEM)],
        scratch_shapes=[
            pltpu.VMEM((9, ROWS, MEMBERS // ROWS, BLOCK), jnp.float32),
            pltpu.VMEM((MEMBERS, 3 * BLOCK), jnp.bfloat16),
            pltpu.VMEM((MEMBERS, 3 * BLOCK), jnp.bfloat16),
            pltpu.VMEM((BLOCK // SUB, SUB, SPAN), jnp.float32),
            pltpu.VMEM((BLOCK // SUB, SUB, SPAN), jnp.bfloat16),
            pltpu.VMEM((BLOCK // SUB, SUB, SPAN), jnp.bfloat16),
            pltpu.VMEM((BLOCK, BLOCK), jnp.float32),
            pltpu.VMEM((STEPS - 1, PIECE, PIECE), jnp.float32),
            pltpu.VMEM((STEPS, 5, PIECE, PIECE), jnp.float32),
            pltpu.VMEM((STEPS, 2, ROWS, PIECE, PIECE), jnp.float32),
            pltpu.VMEM((2 * BLOCK, 2 * PIECE), jnp.bfloat16),
            pltpu.VMEM((STEPS, BLOCK, PIECE), jnp.float32),
            pltpu.VMEM((STEPS, ROWS, PIECE, PIECE), jnp.float32),
            pltpu.VMEM((8, 128), jnp.float32),
            pltpu.VMEM((ROWS, 8, 128), jnp.float32),
            pltpu.VMEM((COLS, 8, 128), jnp.float32),
            pltpu.VMEM((8, 128), jnp.float32),
            pltpu.SemaphoreType.DMA((len(ROUTES), 6)),
            pltpu.SemaphoreType.DMA((len(ROUTES), 6)),
            pltpu.SemaphoreType.DMA,
            pltpu.SemaphoreType.DMA,
            pltpu.SemaphoreType.DMA,
            pltpu.SemaphoreType.DMA((BLOCK // SUB,)),
            pltpu.SemaphoreType.DMA((STEPS, 5)),
            pltpu.SemaphoreType.DMA((STEPS, 5)),
            pltpu.SemaphoreType.DMA((STEPS, 15)),
            pltpu.SemaphoreType.DMA((STEPS, 2, ROWS)),
            pltpu.SemaphoreType.DMA((STEPS, ROWS)),
            pltpu.SemaphoreType.DMA((STEPS, ROWS)),
            pltpu.SemaphoreType.DMA((STEPS, ROWS)),
            pltpu.SemaphoreType.DMA((ROWS,)),
            pltpu.SemaphoreType.DMA((ROWS,)),
            pltpu.SemaphoreType.DMA((COLS,)),
            pltpu.SemaphoreType.DMA((COLS,)),
        ],
        compiler_params=pltpu.CompilerParams(
            collective_id=1, has_side_effects=True, vmem_limit_bytes=VMEM_LIMIT
        ),
    )(members, probes)


def on_device(perturbations, probes):
    return band_and_sample(perturbations, probes)


def solution(mesh):
    return jax.shard_map(
        on_device,
        mesh=mesh,
        in_specs=(P("row", "col"), P(("col", "row"), None)),
        out_specs=(P("col", "row"), P(("col", "row"), None)),
        check_vma=False,
    )
```

time: 180 us -> 133 us (0.74)
  Pallas kernels: 174 us -> 127 us
    pallas_call x1 -> x0, Pallas kernels: 62.8 us -> none  [gathered(): pl.pallas_call(gather_kernel, name='gather_members', out_shape=jax.ShapeD...]
    pallas_call x1, Pallas kernels: 111 us -> 127 us  [band_and_sample(): pl.pallas_call(main_kernel, name='band_and_sample', out_shape=(jax.ShapeD...]
where the time goes in v4:
time: 133 us
  Pallas kernels  127 us (95%)
  local copies, waits for them, and re-layouts  5.45 us (4%)
    pallas_call x1, Pallas kernels, band_and_sample(): pl.pallas_call(main_kernel, name='band_and_sample', out_shape=(jax.ShapeD...  127 us
    unnamed x4, local copies, waits for them, and re-layouts  5.45 us

profile of v4, /device:TPU:26, one launch (start us, length us, event | category | flops | bytes accessed | tf_op | source)
XLA Modules:
  0.0 133.0 jit_solution(6236671756937390053)
XLA Ops:
  0.6 126.9 %band_and_sample.1 = (f32[1024,1024]{1,0:T(8,128)}, f32[128,128]{1,0:T(8,128)}) custom-call(f32[64,1024]{1,0:T(8,128)} %members_ref.1, f32[128,128]{1,0:T(8,128)} %w_ref.1), custom_call_target="tpu_custom_call" | custom-call | tf_op jit(solution)/shard_map/band_and_sample/pallas_call | solution.py:457
  127.5 0.0 copy-start
  127.5 4.8 %copy.6 = f32[1024,1024]{1,0:T(8,128)} copy(f32[1024,1024]{1,0:T(8,128)} %get-tuple-element.4) | data formatting | bytes 8388608
  132.3 0.0 copy-done
  132.3 0.6 copy.7
Async XLA Ops:
  127.5 4.8 %copy-start = (f32[128,128]{1,0:T(8,128)S(1)}, f32[128,128]{1,0:T(8,128)}, u32[]{:S(2)}) copy-start(f32[128,128]{1,0:T(8,128)} %get-tuple-element.5) | copy-start | bytes 196612

commit v5 on v4

--- a/solution.py
+++ b/solution.py
@@ -80,6 +80,7 @@
 DIRECTIONS = ((1, 0, 0), (-1, 0, 0), (0, 1, 0), (0, -1, 0), (0, 0, 1), (0, 0, -1))
 QUARTER = MEMBERS // ROWS // 4
 LAG = 3
+UNITS = 4 * ROWS
 
 
 def place_of(i):
@@ -144,9 +145,10 @@
     sides = [neighbour(d) for d in range(6)]
     other = (r, c + sign)
 
+    own_units = pl.ds(pl.multiple_of((pair * ROWS + r) * 4, 4), 4)
     across = lax.div(lax.rem(2 * pair - 4 + r + 2 - core - lax.rem(r, 2) + COLS, COLS), 2)
 
-    own = pltpu.make_async_copy(x_ref, held.at[pair, r], own_sem)
+    own = pltpu.make_async_copy(x_ref, held.at[own_units], own_sem)
     own.start()
     greet_all(sides)
     own.wait()
@@ -156,8 +158,7 @@
         row = lax.rem(lax.div(entry, 4), 8)
         block = lax.rem(pair + sign * relative + 8, 8)
         row = jnp.where(first, row, 7 - row)
-        quarter = pl.multiple_of(lax.rem(entry, 4) * QUARTER, QUARTER)
-        return block, row, pl.ds(quarter, QUARTER)
+        return block, row * 4 + lax.rem(entry, 4)
 
     def entries(table):
         found = []
@@ -166,24 +167,27 @@
             found += [lax.rem(word, 512), lax.rem(lax.div(word, 512), 512), lax.div(word, 512 * 512)]
         return found
 
-    piece = held.at[pair, r, pl.ds(0, QUARTER)]
-
-    def pass_across(block, row, part):
-        @pl.when(block == across)
-        def _():
-            copied(held.at[block, row, part], held.at[8, row, part], across_send, across_recv, *other).start()
+    def across_copy(mine, there):
+        return copied(held.at[mine], held.at[there], across_send, across_recv, *other)
 
     def take(step):
         for d, entry in enumerate(entries(incoming[step])):
             @pl.when(entry >= 256)
             def _(d=d, entry=entry):
-                block, row, part = unit(entry)
-                ref = held.at[block, row, part]
+                block, number = unit(entry)
+                ref = held.at[block * UNITS + number]
                 pltpu.make_async_copy(ref, ref, recv.at[step, d]).wait()
-                pass_across(block, row, part)
+
+                @pl.when(block == across)
+                def _():
+                    across_copy(block * UNITS + number, 8 * UNITS + number).start()
 
     incoming, outgoing = words(arrivals()), words(departures())
-    pass_across(pair, r, pl.ds(0, MEMBERS // ROWS))
+
+    @pl.when(pair == across)
+    def _():
+        across_copy(own_units, pl.ds(8 * UNITS + r * 4, 4)).start()
+
     rounds = len(ROUTES)
     for step in range(rounds + LAG):
         if step >= LAG:
@@ -192,19 +196,23 @@
             for d, entry in enumerate(entries(outgoing[step])):
                 @pl.when(entry >= 256)
                 def _(d=d, entry=entry):
-                    block, row, part = unit(entry)
-                    ref = held.at[block, row, part]
-                    copied(ref, ref, send.at[step, d], recv.at[step, d], *sides[d]).start()
+                    block, number = unit(entry)
+                    ref = held.at[block * UNITS + number]
+                    copied(ref, ref, send, recv.at[step, d], *sides[d]).start()
+
+    whole = across_copy(pl.ds(0, UNITS), pl.ds(8 * UNITS, UNITS))
+    counts = [sum((packed >> (9 * i) & 256) // 256 for sends in ROUTES for packed in sends) for i in range(32)]
+    count = looked_up(counts, bits)
 
     def finish():
-        for step in range(rounds):
-            for d, entry in enumerate(entries(outgoing[step])):
-                @pl.when(entry >= 256)
-                def _(d=d):
-                    copied(piece, piece, send.at[step, d], recv.at[step, d], *sides[d]).wait_send()
-        copied(held.at[pair], held.at[8], across_send, across_recv, *other).wait_send()
-
-    copied(held.at[pair], held.at[8], across_send, across_recv, *other).wait_recv()
+        for total in sorted(set(counts)):
+            @pl.when(count == total)
+            def _(total=total):
+                units = held.at[pl.ds(0, total)]
+                copied(units, units, send, recv.at[0, 0], *sides[0]).wait_send()
+        whole.wait_send()
+
+    whole.wait_recv()
     return finish
 
 
@@ -231,7 +239,7 @@
     members_ref, w_ref, local_out, out_ref,
     held, xh, xl, band_ref, high_ref, low_ref, local_ref,
     iterate, near, window, wide, parts, sums, square_ref, row_squares, col_squares, row_total,
-    member_send, member_recv, across_send, across_recv, own_sem, store_sem, send_z, recv_z, send_w, recv_w, send_x, send_y, recv_y, send_r, recv_r, send_c, recv_c,
+    member_send, member_recv, across_send, across_recv, own_sem, store_sem, send_z, recv_z, send_w, recv_w, send_x, recv_x, send_y, recv_y, send_r, recv_r, send_c, recv_c,
 ):
     r, c = here()
     core = lax.rem(c, 2)
@@ -254,7 +262,7 @@
 
     def to_pairs(step, source, away):
         col = lax.rem(c - 2 * away + COLS, COLS)
-        return copied(source, near.at[step, away + 2], send_z.at[step, away + 2], recv_z.at[step, away + 2], r, col)
+        return copied(source, near.at[step, away + 2], send_z.at[step], recv_z.at[step, away + 2], r, col)
 
     def targets(away):
         found = []
@@ -271,27 +279,27 @@
                 valid = core == 0 if e == 1 else None
             there = (1, core, 0)[e]
             panel = (1, shared, 0)[e]
-            found.append(((away + 2) * 3 + e, row, there, panel, valid))
+            found.append((row, there, panel, valid))
         return found
 
     def share(step, source, away, act):
-        for slot, row, there, panel, valid in targets(away):
+        for row, there, panel, valid in targets(away):
             own = (row == r) & (there == core)
             go = jnp.logical_not(own)
             if valid is not None:
                 own, go = own & valid, go & valid
 
             @pl.when(go)
-            def _(slot=slot, row=row, there=there, panel=panel):
+            def _(row=row, there=there, panel=panel):
                 act(copied(
-                    source, window.at[step, panel, r], send_w.at[step, slot], recv_w.at[step, panel, r], row, 2 * pair + there
-                ), True)
+                    source, window.at[step, panel, r], send_w.at[step], recv_w.at[step, panel], row, 2 * pair + there
+                ))
 
             @pl.when(own)
             def _(panel=panel):
-                act(pltpu.make_async_copy(source, window.at[step, panel, r], recv_w.at[step, panel, r]), False)
-
-    def begin(copy, remote):
+                act(pltpu.make_async_copy(source, window.at[step, panel, r], recv_w.at[step, panel]))
+
+    def begin(copy):
         copy.start()
 
     def send_iterate(step, source):
@@ -305,32 +313,35 @@
             pltpu.make_async_copy(block, block, recv_z.at[step, away + 2]).wait()
             share(step, block, away, begin)
 
+    def across_copy(step):
+        return copied(
+            window.at[step, shared], window.at[step, 1 - shared], send_x.at[step], recv_x.at[step], *other
+        )
+
+    def split(step, panel):
+        high, low = parted(window[step, panel].reshape(BLOCK, PIECE))
+        first = pl.multiple_of(panel * BLOCK, BLOCK)
+        wide[pl.ds(first, BLOCK), :PIECE] = high
+        wide[pl.ds(first, BLOCK), PIECE:] = low
+
+    def landed(step, panel):
+        block = window.at[step, panel]
+        pltpu.make_async_copy(block, block, recv_w.at[step, panel]).wait()
+
     def take_iterate(step):
         @pl.when(passes)
         def _():
-            for row in range(ROWS):
-                block = window.at[step, shared, row]
-                pltpu.make_async_copy(block, block, recv_w.at[step, shared, row]).wait()
-                there = window.at[step, 1 - shared, row]
-                copied(block, there, send_x.at[step, row], recv_w.at[step, 1 - shared, row], *other).start()
-                split(step, shared, row)
-        for row in range(ROWS):
-            landed(step, core, row)
+            landed(step, shared)
+            across_copy(step).start()
+            split(step, shared)
+
+        landed(step, core)
+        split(step, core)
+
         @pl.when(jnp.logical_not(passes))
         def _():
-            for row in range(ROWS):
-                landed(step, shared, row)
-
-    def split(step, panel, row):
-        high, low = parted(window[step, panel, row])
-        first = pl.multiple_of((panel * ROWS + row) * PIECE, PIECE)
-        wide[pl.ds(first, PIECE), :PIECE] = high
-        wide[pl.ds(first, PIECE), PIECE:] = low
-
-    def landed(step, panel, row):
-        block = window.at[step, panel, row]
-        pltpu.make_async_copy(block, block, recv_w.at[step, panel, row]).wait()
-        split(step, panel, row)
+            across_copy(step).wait_recv()
+            split(step, shared)
 
     finish = gather_members(
         members_ref, held, member_send, member_recv, across_send, across_recv, own_sem, greet_all
@@ -343,7 +354,7 @@
     odd = lax.rem(r, 2) == 1
     for panel, block in enumerate((pair, jnp.where(odd, 8, near_block), jnp.where(odd, far_block, 8))):
         for first in range(0, BLOCK, SUB):
-            values = held[block, :, :, first : first + SUB].reshape(MEMBERS, SUB)
+            values = held[pl.ds(block * UNITS, UNITS), :, first : first + SUB].reshape(MEMBERS, SUB)
             centered = values - jnp.sum(values, 0, keepdims=True) / MEMBERS
             spread = jnp.sqrt(jnp.sum(centered * centered, 0, keepdims=True) + epsilon)
             high, low = parted(centered / spread)
@@ -371,8 +382,7 @@
     square_ref[...] = squares
 
     for shift in range(1, ROWS):
-        copied(square_ref, row_squares.at[r], send_r.at[shift], recv_r.at[r], lax.rem(r + shift, ROWS), c).start()
-    pltpu.make_async_copy(square_ref, row_squares.at[r], recv_r.at[r]).start()
+        copied(square_ref, row_squares.at[r], send_r, recv_r, lax.rem(r + shift, ROWS), c).start()
 
     stores = []
 
@@ -383,6 +393,25 @@
         stores.append(pltpu.make_async_copy(local_ref.at[first : first + SUB], local_out.at[first : first + SUB], store_sem.at[tile]))
         stores[-1].start()
 
+    def several(ref, send, recv):
+        return copied(ref, ref, send, recv, *other)
+
+    def piece_out(step, row):
+        return copied(
+            parts.at[step, row * PIECE : (row + 1) * PIECE], sums.at[step * ROWS + r],
+            send_y.at[step], recv_y.at[step], row, c,
+        )
+
+    def sent(step):
+        several(near.at[step, pl.ds(0, 4)], send_z.at[step], recv_z.at[step, 0]).wait_send()
+        several(sums.at[pl.ds(0, 11)], send_w.at[step], recv_w.at[step, 0]).wait_send()
+        pl.when(passes)(lambda: across_copy(step).wait_send())
+
+    def pieces(step):
+        return several(sums.at[pl.ds(step * ROWS, ROWS - 1)], send_y.at[step], recv_y.at[step])
+
+    row_copies = several(row_squares.at[pl.ds(0, ROWS - 1)], send_r, recv_r)
+    col_copies = several(col_squares.at[pl.ds(0, COLS - 1)], send_c, recv_c)
     total = None
     summed = power_terms[0] * w_ref[...]
     for step in range(STEPS):
@@ -394,63 +423,50 @@
             rest = dotted(low_ref[tile], wide[first : first + SPAN, :PIECE], over)
             parts[step, first : first + SUB, :] = both[:, :PIECE] + (both[:, PIECE:] + rest)
             for row in range(first // PIECE, (first + SUB) // PIECE):
-                def go(row=row):
-                    copied(
-                        parts.at[step, row * PIECE : (row + 1) * PIECE], sums.at[step, r],
-                        send_y.at[step, row], recv_y.at[step, r], row, c,
-                    ).start()
-
-                unless(r == row, go)
+                unless(r == row, lambda row=row: piece_out(step, row).start())
         if step == 0:
+            row_copies.wait_recv()
+            squares = jnp.zeros((8, 128), jnp.float32)
             for row in range(ROWS):
-                pltpu.make_async_copy(square_ref, row_squares.at[row], recv_r.at[row]).wait()
-            row_total[...] = jnp.sum(row_squares[...], 0)
+                squares = squares + jnp.where(r == row, square_ref[...], row_squares[row])
+            row_total[...] = squares
             for shift in range(1, COLS):
-                copied(row_total, col_squares.at[c], send_c.at[shift], recv_c.at[c], r, lax.rem(c + shift, COLS)).start()
-            pltpu.make_async_copy(row_total, col_squares.at[c], recv_c.at[c]).start()
-        if step < 2:
-            skew(2 * step)
-        if step == 0:
+                copied(row_total, col_squares.at[c], send_c, recv_c, r, lax.rem(c + shift, COLS)).start()
+            skew(0)
+            col_copies.wait_recv()
+            squares = jnp.zeros((8, 128), jnp.float32)
             for col in range(COLS):
-                pltpu.make_async_copy(row_total, col_squares.at[col], recv_c.at[col]).wait()
-            total = jnp.sum(jnp.sum(col_squares[...], 0), keepdims=True) / STATES
+                squares = squares + jnp.where(c == col, row_total[...], col_squares[col])
+            total = jnp.sum(squares, keepdims=True) / STATES
+        elif step == 1:
+            skew(2)
+        else:
+            sent(1)
+            sent(2)
+            pieces(0).wait_send()
+            pieces(1).wait_send()
         vector = parts[step, pl.ds(pl.multiple_of(r * PIECE, PIECE), PIECE), :]
+        pieces(step).wait_recv()
         for row in range(ROWS):
-            def arrived(row=row):
-                pltpu.make_async_copy(w_ref, sums.at[step, row], recv_y.at[step, row]).wait()
-
-            unless(r == row, arrived)
-            vector = vector + jnp.where(r == row, 0.0, sums[step, row])
+            vector = vector + jnp.where(r == row, 0.0, sums[step * ROWS + row])
         vector = vector / total
         summed = summed + power_terms[step + 1] * vector
         if step < STEPS - 1:
             iterate[step] = vector
             send_iterate(step + 1, iterate.at[step])
+            if step == 0:
+                finish()
+                sent(0)
+            else:
+                row_copies.wait_send()
+                col_copies.wait_send()
             spread_iterate(step + 1)
             skew(2 * step + 1)
     out_ref[...] = jnp.sqrt(total) * summed
 
     for copy in stores:
         copy.wait()
-    finish()
-    for shift in range(1, ROWS):
-        copied(square_ref, row_squares.at[r], send_r.at[shift], recv_r.at[r], lax.rem(r + shift, ROWS), c).wait_send()
-    for shift in range(1, COLS):
-        copied(row_total, col_squares.at[c], send_c.at[shift], recv_c.at[c], r, lax.rem(c + shift, COLS)).wait_send()
-    for step in range(STEPS):
-        for away in (-2, -1, 1, 2):
-            to_pairs(step, w_ref, away).wait_send()
-        for away in range(-2, 3):
-            share(step, w_ref, away, lambda copy, remote: copy.wait_send() if remote else None)
-        @pl.when(passes)
-        def _(step=step):
-            for row in range(ROWS):
-                copied(w_ref, window.at[step, core, row], send_x.at[step, row], recv_w.at[step, core, row], *other).wait_send()
-        for row in range(ROWS):
-            def gone(row=row):
-                copied(w_ref, sums.at[step, r], send_y.at[step, row], recv_y.at[step, r], row, c).wait_send()
-
-            unless(r == row, gone)
+    pieces(STEPS - 1).wait_send()
 
 
 def band_and_sample(members, probes):
@@ -464,7 +480,7 @@
         in_specs=[pl.BlockSpec(memory_space=pl.ANY), pl.BlockSpec(memory_space=pltpu.VMEM)],
         out_specs=[pl.BlockSpec(memory_space=pl.ANY), pl.BlockSpec(memory_space=pltpu.VMEM)],
         scratch_shapes=[
-            pltpu.VMEM((9, ROWS, MEMBERS // ROWS, BLOCK), jnp.float32),
+            pltpu.VMEM((9 * UNITS, QUARTER, BLOCK), jnp.float32),
             pltpu.VMEM((MEMBERS, 3 * BLOCK), jnp.bfloat16),
             pltpu.VMEM((MEMBERS, 3 * BLOCK), jnp.bfloat16),
             pltpu.VMEM((BLOCK // SUB, SUB, SPAN), jnp.float32),
@@ -476,28 +492,29 @@
             pltpu.VMEM((STEPS, 2, ROWS, PIECE, PIECE), jnp.float32),
             pltpu.VMEM((2 * BLOCK, 2 * PIECE), jnp.bfloat16),
             pltpu.VMEM((STEPS, BLOCK, PIECE), jnp.float32),
-            pltpu.VMEM((STEPS, ROWS, PIECE, PIECE), jnp.float32),
+            pltpu.VMEM((STEPS * ROWS, PIECE, PIECE), jnp.float32),
             pltpu.VMEM((8, 128), jnp.float32),
             pltpu.VMEM((ROWS, 8, 128), jnp.float32),
             pltpu.VMEM((COLS, 8, 128), jnp.float32),
             pltpu.VMEM((8, 128), jnp.float32),
+            pltpu.SemaphoreType.DMA,
             pltpu.SemaphoreType.DMA((len(ROUTES), 6)),
-            pltpu.SemaphoreType.DMA((len(ROUTES), 6)),
             pltpu.SemaphoreType.DMA,
             pltpu.SemaphoreType.DMA,
             pltpu.SemaphoreType.DMA,
             pltpu.SemaphoreType.DMA((BLOCK // SUB,)),
+            pltpu.SemaphoreType.DMA((STEPS,)),
             pltpu.SemaphoreType.DMA((STEPS, 5)),
-            pltpu.SemaphoreType.DMA((STEPS, 5)),
-            pltpu.SemaphoreType.DMA((STEPS, 15)),
-            pltpu.SemaphoreType.DMA((STEPS, 2, ROWS)),
-            pltpu.SemaphoreType.DMA((STEPS, ROWS)),
-            pltpu.SemaphoreType.DMA((STEPS, ROWS)),
-            pltpu.SemaphoreType.DMA((STEPS, ROWS)),
-            pltpu.SemaphoreType.DMA((ROWS,)),
-            pltpu.SemaphoreType.DMA((ROWS,)),
-            pltpu.SemaphoreType.DMA((COLS,)),
-            pltpu.SemaphoreType.DMA((COLS,)),
+            pltpu.SemaphoreType.DMA((STEPS,)),
+            pltpu.SemaphoreType.DMA((STEPS, 2)),
+            pltpu.SemaphoreType.DMA((STEPS,)),
+            pltpu.SemaphoreType.DMA((STEPS,)),
+            pltpu.SemaphoreType.DMA((STEPS,)),
+            pltpu.SemaphoreType.DMA((STEPS,)),
+            pltpu.SemaphoreType.DMA,
+            pltpu.SemaphoreType.DMA,
+            pltpu.SemaphoreType.DMA,
+            pltpu.SemaphoreType.DMA,
         ],
         compiler_params=pltpu.CompilerParams(
             collective_id=1, has_side_effects=True, vmem_limit_bytes=VMEM_LIMIT
@@ -506,7 +523,7 @@
 
 
 def on_device(perturbations, probes):
-    return band_and_sample(perturbations, probes)
+    return band_and_sample(perturbations.reshape(4, QUARTER, BLOCK), probes)
 
 
 def solution(mesh):

time: 133 us -> 131 us (0.985)
  Pallas kernels: 127 us -> 124 us
    pallas_call x1, Pallas kernels: 127 us -> 124 us  [band_and_sample(): pl.pallas_call(main_kernel, name='band_and_sample', out_shape=(jax.ShapeD...]
where the time goes in v5:
time: 131 us
  Pallas kernels  124 us (95%)
  local copies, waits for them, and re-layouts  5.45 us (4%)
    pallas_call x1, Pallas kernels, band_and_sample(): pl.pallas_call(main_kernel, name='band_and_sample', out_shape=(jax.ShapeD...  124 us
    unnamed x4, local copies, waits for them, and re-layouts  5.45 us

profile of v5, /device:TPU:26, one launch (start us, length us, event | category | flops | bytes accessed | tf_op | source)
XLA Modules:
  0.0 130.5 jit_solution(5879578886518848227)
XLA Ops:
  0.6 124.4 %band_and_sample.1 = (f32[1024,1024]{1,0:T(8,128)}, f32[128,128]{1,0:T(8,128)}) custom-call(f32[4,16,1024]{2,1,0:T(8,128)} %bitcast.1, f32[128,128]{1,0:T(8,128)} %w_ref.1), custom_call_target="tpu_custom_call" | custom-call | tf_op jit(solution)/shard_map/band_and_sample/pallas_call | solution.py:473
  125.1 0.0 copy-start
  125.1 4.8 %copy.6 = f32[1024,1024]{1,0:T(8,128)} copy(f32[1024,1024]{1,0:T(8,128)} %get-tuple-element.4) | data formatting | bytes 8388608
  129.9 0.0 copy-done
  129.9 0.6 copy.7
Async XLA Ops:
  125.1 4.8 %copy-start = (f32[128,128]{1,0:T(8,128)S(1)}, f32[128,128]{1,0:T(8,128)}, u32[]{:S(2)}) copy-start(f32[128,128]{1,0:T(8,128)} %get-tuple-element.5) | copy-start | bytes 196612

commit v6 on v5

--- a/solution.py
+++ b/solution.py
@@ -522,8 +522,45 @@
     )(members, probes)
 
 
+def hand_over_kernel(local_ref, sampled_ref, local_out, sampled_out, held, held_sampled, load_sem, store_sem):
+    parts = BLOCK // SUB
+    moves = []
+    for source, middle, target, n in [(sampled_ref, held_sampled, sampled_out, parts)] + [
+        (*(ref.at[n * SUB : (n + 1) * SUB] for ref in (local_ref, held, local_out)), n) for n in range(parts)
+    ]:
+        load = pltpu.make_async_copy(source, middle, load_sem.at[n])
+        load.start()
+        moves.append((load, pltpu.make_async_copy(middle, target, store_sem.at[n])))
+    for load, store in moves:
+        load.wait()
+        store.start()
+    for _, store in moves:
+        store.wait()
+
+
+def handed_over(localized, sampled):
+    parts = BLOCK // SUB + 1
+    return pl.pallas_call(
+        hand_over_kernel,
+        name="hand_over",
+        out_shape=(
+            jax.ShapeDtypeStruct((BLOCK, BLOCK), jnp.float32),
+            jax.ShapeDtypeStruct((PIECE, PIECE), jnp.float32),
+        ),
+        in_specs=[pl.BlockSpec(memory_space=pl.ANY)] * 2,
+        out_specs=[pl.BlockSpec(memory_space=pl.ANY)] * 2,
+        scratch_shapes=[
+            pltpu.VMEM((BLOCK, BLOCK), jnp.float32),
+            pltpu.VMEM((PIECE, PIECE), jnp.float32),
+            pltpu.SemaphoreType.DMA((parts,)),
+            pltpu.SemaphoreType.DMA((parts,)),
+        ],
+        compiler_params=pltpu.CompilerParams(vmem_limit_bytes=16 * 2**20),
+    )(localized, sampled)
+
+
 def on_device(perturbations, probes):
-    return band_and_sample(perturbations.reshape(4, QUARTER, BLOCK), probes)
+    return handed_over(*band_and_sample(perturbations.reshape(4, QUARTER, BLOCK), probes))
 
 
 def solution(mesh):

time: 131 us -> 131 us (level)
  Pallas kernels: 124 us -> 127 us
  local copies, waits for them, and re-layouts: 5.45 us -> 3.02 us
    pallas_call x0 -> x1, Pallas kernels: none -> 2.45 us  [handed_over(): pl.pallas_call(hand_over_kernel, name='hand_over', out_shape=(jax.ShapeDt...]
    unnamed x4, local copies, waits for them, and re-layouts: 5.45 us -> 3.02 us
where the time goes in v6:
time: 131 us
  Pallas kernels  127 us (97%)
  local copies, waits for them, and re-layouts  3.02 us (2%)
    pallas_call x1, Pallas kernels, band_and_sample(): pl.pallas_call(main_kernel, name='band_and_sample', out_shape=(jax.ShapeD...  124 us
    unnamed x4, local copies, waits for them, and re-layouts  3.02 us

profile of v6, /device:TPU:26, one launch (start us, length us, event | category | flops | bytes accessed | tf_op | source)
XLA Modules:
  0.0 130.7 jit_solution(4666866103819327101)
XLA Ops:
  0.6 124.4 %band_and_sample.1 = (f32[1024,1024]{1,0:T(8,128)}, f32[128,128]{1,0:T(8,128)}) custom-call(f32[4,16,1024]{2,1,0:T(8,128)} %bitcast.1, f32[128,128]{1,0:T(8,128)} %w_ref.1), custom_call_target="tpu_custom_call" | custom-call | tf_op jit(solution)/shard_map/band_and_sample/pallas_call | solution.py:473
  125.0 0.0 copy-start
  125.1 2.2 %copy-done = f32[1024,1024]{1,0:T(8,128)S(1)} copy-done((f32[1024,1024]{1,0:T(8,128)S(1)}, f32[1024,1024]{1,0:T(8,128)}, u32[]{:S(2)}) %copy-start) | copy-done | bytes 4194328
  127.2 0.0 copy-start.1
  127.2 0.8 copy-done.1
  128.1 2.4 %hand_over.1 = (f32[1024,1024]{1,0:T(8,128)}, f32[128,128]{1,0:T(8,128)}) custom-call(f32[1024,1024]{1,0:T(8,128)S(1)} %copy-done, f32[128,128]{1,0:T(8,128)S(1)} %copy-done.1), custom_call_target="tpu_custom_call" | custom-call | tf_op jit(solution)/shard_map/hand_over/pallas_call | solution.py:543
Async XLA Ops:
  125.0 2.2 %copy-start = (f32[1024,1024]{1,0:T(8,128)S(1)}, f32[1024,1024]{1,0:T(8,128)}, u32[]{:S(2)}) copy-start(f32[1024,1024]{1,0:T(8,128)} %get-tuple-element.4.local_ref) | copy-start | bytes 12582916
  127.2 0.8 copy-start.1

commit v7 on v5

--- a/solution.py
+++ b/solution.py
@@ -125,7 +125,7 @@
     return jnp.where(bits[-1], high, low)
 
 
-def gather_members(x_ref, held, send, recv, across_send, across_recv, own_sem, greet_all):
+def gather_members(x_ref, held, send, recv, across_send, across_recv, own_sem, greet_all, before, spread_early, beside):
     r, c = here()
     core = lax.rem(c, 2)
     pair = lax.div(c, 2)
@@ -152,6 +152,7 @@
     own.start()
     greet_all(sides)
     own.wait()
+    before()
 
     def unit(entry):
         relative = lax.rem(lax.div(entry, 32), 8)
@@ -190,6 +191,8 @@
 
     rounds = len(ROUTES)
     for step in range(rounds + LAG):
+        if step == rounds:
+            spread_early()
         if step >= LAG:
             take(step - LAG)
         if step < rounds:
@@ -212,6 +215,7 @@
                 copied(units, units, send, recv.at[0, 0], *sides[0]).wait_send()
         whole.wait_send()
 
+    beside()
     whole.wait_recv()
     return finish
 
@@ -343,16 +347,7 @@
             across_copy(step).wait_recv()
             split(step, shared)
 
-    finish = gather_members(
-        members_ref, held, member_send, member_recv, across_send, across_recv, own_sem, greet_all
-    )
-    send_iterate(0, w_ref)
-    spread_iterate(0)
-
-    near_block = lax.div(lax.rem(c + r - 4 + COLS, COLS), 2)
-    far_block = lax.div(lax.rem(c + r - 3 + COLS, COLS), 2)
-    odd = lax.rem(r, 2) == 1
-    for panel, block in enumerate((pair, jnp.where(odd, 8, near_block), jnp.where(odd, far_block, 8))):
+    def normalise(panel, block):
         for first in range(0, BLOCK, SUB):
             values = held[pl.ds(block * UNITS, UNITS), :, first : first + SUB].reshape(MEMBERS, SUB)
             centered = values - jnp.sum(values, 0, keepdims=True) / MEMBERS
@@ -361,6 +356,16 @@
             lo_at = (panel - 1) * BLOCK + first if panel else 2 * BLOCK + first
             xh[:, lo_at : lo_at + SUB] = high
             xl[:, lo_at : lo_at + SUB] = low
+
+    finish = gather_members(
+        members_ref, held, member_send, member_recv, across_send, across_recv, own_sem, greet_all,
+        lambda: send_iterate(0, w_ref), lambda: spread_iterate(0), lambda: normalise(0, pair),
+    )
+    near_block = lax.div(lax.rem(c + r - 4 + COLS, COLS), 2)
+    far_block = lax.div(lax.rem(c + r - 3 + COLS, COLS), 2)
+    odd = lax.rem(r, 2) == 1
+    normalise(1, jnp.where(odd, 8, near_block))
+    normalise(2, jnp.where(odd, far_block, 8))
     squares = jnp.zeros((8, 128), jnp.float32)
     gap = lax.broadcasted_iota(jnp.int32, (SUB, SPAN), 1) - lax.broadcasted_iota(jnp.int32, (SUB, SPAN), 0)
     taper = jnp.maximum(0.0, 1.0 - jnp.abs(gap + (r * BLOCK - WINDOW)).astype(jnp.float32) / WINDOW)

time: 131 us -> 126 us (0.962)
  Pallas kernels: 124 us -> 120 us
    pallas_call x1, Pallas kernels: 124 us -> 120 us  [band_and_sample(): pl.pallas_call(main_kernel, name='band_and_sample', out_shape=(jax.ShapeD...]
where the time goes in v7:
time: 126 us
  Pallas kernels  120 us (95%)
  local copies, waits for them, and re-layouts  5.45 us (4%)
    pallas_call x1, Pallas kernels, band_and_sample(): pl.pallas_call(main_kernel, name='band_and_sample', out_shape=(jax.ShapeD...  120 us
    unnamed x4, local copies, waits for them, and re-layouts  5.45 us

profile of v7, /device:TPU:26, one launch (start us, length us, event | category | flops | bytes accessed | tf_op | source)
XLA Modules:
  0.0 126.1 jit_solution(17982122770094470344)
XLA Ops:
  0.6 120.0 %band_and_sample.1 = (f32[1024,1024]{1,0:T(8,128)}, f32[128,128]{1,0:T(8,128)}) custom-call(f32[4,16,1024]{2,1,0:T(8,128)} %bitcast.1, f32[128,128]{1,0:T(8,128)} %w_ref.1), custom_call_target="tpu_custom_call" | custom-call | tf_op jit(solution)/shard_map/band_and_sample/pallas_call | solution.py:478
  120.6 0.0 copy-start
  120.7 4.8 %copy.6 = f32[1024,1024]{1,0:T(8,128)} copy(f32[1024,1024]{1,0:T(8,128)} %get-tuple-element.4) | data formatting | bytes 8388608
  125.5 0.0 copy-done
  125.5 0.6 copy.7
Async XLA Ops:
  120.6 4.8 %copy-start = (f32[128,128]{1,0:T(8,128)S(1)}, f32[128,128]{1,0:T(8,128)}, u32[]{:S(2)}) copy-start(f32[128,128]{1,0:T(8,128)} %get-tuple-element.5) | copy-start | bytes 196612
